TPU v7x, 256 devices: a whole 4x4x8 slice. The times are simulated.
256 devices in a mesh: dp: 16 (over x_hi, z), mp: 16 (over x_lo, y, core).
Axes of the slice: x: 4 (x_hi: 2, x_lo: 2; x = x_hi * 2 + x_lo), y: 4, z: 8, core: 2. Of those that a mesh axis runs over, the one named last changes fastest.
Arguments:
- inputs: bfloat16 [6144, 4096], P('dp', 'mp'), may hold values from -6 to 6
- out_cotangent: bfloat16 [6144, 4096], P('dp'), may hold values from -6 to 6
- gate_weight: bfloat16 [4096, 6144], P('dp', 'mp'), may hold values from -0.09375 to 0.09375
- linear_weight: bfloat16 [4096, 6144], P('dp', 'mp'), may hold values from -0.09375 to 0.09375
- output_weight: bfloat16 [6144, 4096], P('mp', 'dp'), may hold values from -0.078125 to 0.078125
Outputs:
- layer_output: bfloat16 [6144, 4096], P('dp', 'mp')
- input_grad: bfloat16 [6144, 4096], P('dp', 'mp')
- gate_grad: float32 [4096, 6144], P('dp', 'mp')
- linear_grad: float32 [4096, 6144], P('dp', 'mp')
- output_grad: float32 [6144, 4096], P('mp', 'dp')
All inputs are finite; a program needn't handle non-finite values.
Results may differ from a plain program's by a relative error of at most 0.023.
Values may be sent and summed in bfloat16 or wider, within the bound.
No kernel may reach another device: no remote copies, remote signals or barrier semaphores. Data moves between devices by JAX's collectives and lax.ppermute only.
A program may use at most 128 MiB of HBM per device.

v0:
```python
import jax
import jax.numpy as jnp
from jax import lax
from jax.sharding import PartitionSpec as P


def gelu_tanh(values):
    return jax.nn.gelu(values, approximate=True)


def per_device(inputs, out_cotangent, gate_weight, linear_weight, output_weight):
    features = lax.all_gather(inputs, "mp", axis=1, tiled=True)
    width = gate_weight.shape[1]
    gate_full, linear_full = (
        lax.all_gather(gate_weight, "dp", axis=0, tiled=True),
        lax.all_gather(linear_weight, "dp", axis=0, tiled=True),
    )
    gate = jnp.dot(features, gate_full, preferred_element_type=jnp.float32)
    linear = jnp.dot(features, linear_full, preferred_element_type=jnp.float32)
    out_full = lax.all_gather(output_weight, "dp", axis=1, tiled=True)
    activated, gelu_back = jax.vjp(gelu_tanh, gate)
    hidden = (activated * linear).astype(jnp.bfloat16)
    out_terms = jnp.dot(hidden, out_full, preferred_element_type=jnp.float32)
    layer_output = lax.psum_scatter(
        out_terms.astype(jnp.bfloat16), "mp", scatter_dimension=1, tiled=True
    )
    hidden_cot = lax.dot_general(
        out_cotangent, out_full, (((1,), (1,)), ((), ())), preferred_element_type=jnp.float32
    )
    gate_cot = gelu_back(hidden_cot * linear)[0].astype(jnp.bfloat16)
    linear_cot = (hidden_cot * activated).astype(jnp.bfloat16)
    dimension = (((1,), (1,)), ((), ()))
    in_terms = lax.dot_general(gate_cot, gate_full, dimension, preferred_element_type=jnp.float32)
    in_terms = in_terms + lax.dot_general(
        linear_cot, linear_full, dimension, preferred_element_type=jnp.float32
    )
    input_grad = lax.psum_scatter(
        in_terms.astype(jnp.bfloat16), "mp", scatter_dimension=1, tiled=True
    )
    both_cot = jnp.concatenate([gate_cot, linear_cot], axis=1)
    contract = (((0,), (0,)), ((), ()))
    in_grads = lax.dot_general(features, both_cot, contract, preferred_element_type=jnp.float32)
    in_share = lax.psum_scatter(
        in_grads.astype(jnp.bfloat16), "dp", scatter_dimension=0, tiled=True
    ).astype(jnp.float32)
    out_grads = lax.dot_general(hidden, out_cotangent, contract, preferred_element_type=jnp.float32)
    output_grad = lax.psum_scatter(
        out_grads.astype(jnp.bfloat16), "dp", scatter_dimension=1, tiled=True
    ).astype(jnp.float32)
    gate_grad = in_share[:, :width]
    linear_grad = in_share[:, width:]
    return (layer_output, input_grad, gate_grad, linear_grad, output_grad)


def solution(mesh):
    return jax.shard_map(
        per_device,
        mesh=mesh,
        in_specs=(P("dp", "mp"), P("dp", None), P("dp", "mp"), P("dp", "mp"), P("mp", "dp")),
        out_specs=(P("dp", "mp"), P("dp", "mp"), P("dp", "mp"), P("dp", "mp"), P("mp", "dp")),
        check_vma=False,
    )
```

profile of v0, /device:TPU:1, one launch (start us, length us, event | category | flops | bytes accessed | tf_op | source)
XLA Modules:
  0.0 919.8 jit_solution(18142237115292020153)
XLA Ops:
  7.2 0.7 all-gather.5.cloned.1.call-update
  8.0 0.7 all-gather.7.cloned.1.call-update
  8.7 0.7 all-gather.9.cloned.1.call-update
  9.4 0.5 all-gather.11.cloned.1.call-update
  10.0 48.2 %all-gather.5.cloned.1.call-done = bf16[384,4096]{1,0:T(8,128)(2,1)} async-done(((bf16[384,256]{1,0:T(8,128)(2,1)}), bf16[384,4096]{1,0:T(8,128)(2,1)}) %all-gather.5.cloned.1.call-update) | async-done | bytes 3145744 | tf_op jit(solution)/shard_map/all_gather | solution.py:12
  58.3 91.7 %all-gather.7.cloned.1.call-done = bf16[4096,384]{1,0:T(8,128)(2,1)} async-done(((bf16[256,384]{1,0:T(8,128)(2,1)}), bf16[4096,384]{1,0:T(8,128)(2,1)}) %all-gather.7.cloned.1.call-update) | async-done | bytes 3145744 | tf_op jit(solution)/shard_map/all_gather | solution.py:15
  150.0 5.5 fusion.13
  155.5 87.0 %all-gather.9.cloned.1.call-done = bf16[4096,384]{1,0:T(8,128)(2,1)} async-done(((bf16[256,384]{1,0:T(8,128)(2,1)}), bf16[4096,384]{1,0:T(8,128)(2,1)}) %all-gather.9.cloned.1.call-update) | async-done | bytes 3145744 | tf_op jit(solution)/shard_map/all_gather | solution.py:16
  242.5 5.5 fusion.14
  248.0 89.0 %all-gather.11.cloned.1.call-done = bf16[384,4096]{1,0:T(8,128)(2,1)} async-done(((bf16[384,256]{1,0:T(8,128)(2,1)}), bf16[384,4096]{1,0:T(8,128)(2,1)}) %all-gather.11.cloned.1.call-update) | async-done | bytes 3145744 | tf_op jit(solution)/shard_map/all_gather | solution.py:20
  337.0 5.1 multiply_convert_fusion
  342.1 3.5 convolution_convert_fusion.1
  345.7 8.2 fusion
  353.9 5.4 convolution_convert_fusion.2
  359.6 4.0 fusion.15
  363.6 3.6 add_convert_fusion
  367.1 184.2 %reduce-scatter.11.cloned.1.call-done = bf16[384,256]{1,0:T(8,128)(2,1)} async-done(((bf16[384,4096]{1,0:T(8,128)(2,1)}), bf16[384,256]{1,0:T(8,128)(2,1)}) %reduce-scatter.11.cloned.1.call-update) | async-done | bytes 196624 | tf_op jit(solution)/shard_map/reduce_scatter | solution.py:47
  551.3 1.7 convert_element_type.39
  553.0 221.3 %reduce-scatter.9.cloned.1.call-done = bf16[256,768]{0,1:T(8,128)(2,1)} async-done(((bf16[4096,768]{0,1:T(8,128)(2,1)}), bf16[256,768]{0,1:T(8,128)(2,1)}) %reduce-scatter.9.cloned.1.call-update) | async-done | bytes 393232 | tf_op jit(solution)/shard_map/reduce_scatter | solution.py:43
  774.4 1.8 fusion.12
  776.2 1.9 copy.10
  778.1 0.9 copy.11
  779.0 64.7 %reduce-scatter.5.cloned.1.call-done = bf16[384,256]{1,0:T(8,128)(2,1)} async-done(((bf16[384,4096]{1,0:T(8,128)(2,1)}), bf16[384,256]{1,0:T(8,128)(2,1)}) %reduce-scatter.5.cloned.1.call-update) | async-done | bytes 196624 | tf_op jit(solution)/shard_map/reduce_scatter | solution.py:24
  843.6 69.3 %reduce-scatter.7.cloned.1.call-done = bf16[384,256]{1,0:T(8,128)(2,1)} async-done(((bf16[384,4096]{1,0:T(8,128)(2,1)}), bf16[384,256]{1,0:T(8,128)(2,1)}) %reduce-scatter.7.cloned.1.call-update) | async-done | bytes 196624 | tf_op jit(solution)/shard_map/reduce_scatter | solution.py:37
  (18 shorter events, 0.6 us)
Async XLA Ops:
  7.2 329.8 %copy-start = (bf16[384,4096]{1,0:T(8,128)(2,1)S(1)}, bf16[384,4096]{1,0:T(8,128)(2,1)}, u32[]{:S(2)}) copy-start(bf16[384,4096]{1,0:T(8,128)(2,1)} %param.6) | copy-start | bytes 9437188
  7.2 51.1 %all-gather.5.cloned.1.call-start = ((), (), s32[]{:S(2)}) async-start(), calls=%async_computation.4 | async-start | bytes 3342336 | tf_op jit(solution)/shard_map/all_gather | solution.py:12
  7.9 142.1 %all-gather.7.cloned.1.call-start = ((), (), s32[]{:S(2)}) async-start(), calls=%async_computation.5 | async-start | bytes 3342336 | tf_op jit(solution)/shard_map/all_gather | solution.py:15
  8.7 233.9 %all-gather.9.cloned.1.call-start = ((), (), s32[]{:S(2)}) async-start(), calls=%async_computation.6 | async-start | bytes 3342336 | tf_op jit(solution)/shard_map/all_gather | solution.py:16
  9.4 327.6 %all-gather.11.cloned.1.call-start = ((), (), s32[]{:S(2)}) async-start(), calls=%async_computation.7 | async-start | bytes 3342336 | tf_op jit(solution)/shard_map/all_gather | solution.py:20
  10.0 541.4 %reduce-scatter.11.cloned.1.call-start = ((), (), s32[]{:S(2)}) async-start(), calls=%async_computation.11 | async-start | bytes 3342336 | tf_op jit(solution)/shard_map/reduce_scatter | solution.py:47
  345.6 428.7 %reduce-scatter.9.cloned.1.call-start = ((), (), s32[]{:S(2)}) async-start(), calls=%async_computation.10 | async-start | bytes 6684672 | tf_op jit(solution)/shard_map/reduce_scatter | solution.py:43
  353.9 489.8 %reduce-scatter.5.cloned.1.call-start = ((), (), s32[]{:S(2)}) async-start(), calls=%async_computation.8 | async-start | bytes 3342336 | tf_op jit(solution)/shard_map/reduce_scatter | solution.py:24
  359.3 4.2 copy-start.2
  359.3 553.6 %reduce-scatter.7.cloned.1.call-start = ((), (), s32[]{:S(2)}) async-start(), calls=%async_computation.9 | async-start | bytes 3342336 | tf_op jit(solution)/shard_map/reduce_scatter | solution.py:37
  359.5 4.0 copy-start.1
Sparse Core Ops, SparseCore 0:
  9.8 48.4 all-gather.4
  60.8 89.0 all-gather.6
  152.6 89.9 all-gather.8
  244.8 92.1 all-gather.10
  345.7 205.5 reduce-scatter.10
  555.9 218.3 reduce-scatter.8
  777.5 66.1 reduce-scatter.4
  846.8 66.1 reduce-scatter.6
where the time goes:
time: 922 us; the launch traced here: 920 us
  waiting for transfers between devices  858 us (93%)
  matrix products  40.7 us (4%)
  between operations  14.2 us (2%)
    reduce_scatter x1, waiting for transfers between devices, per_device(): lax.psum_scatter(in_grads.astype(jnp.bfloat16), 'dp', scatter_dimension=0...  221 us
    reduce_scatter x1, waiting for transfers between devices, per_device(): lax.psum_scatter(out_grads.astype(jnp.bfloat16), 'dp', scatter_dimension=...  184 us
    all_gather x1, waiting for transfers between devices, per_device(): lax.all_gather(gate_weight, 'dp', axis=0, tiled=True)  91.7 us
    all_gather x1, waiting for transfers between devices, per_device(): out_full = lax.all_gather(output_weight, 'dp', axis=1, tiled=True)  89 us
    all_gather x1, waiting for transfers between devices, per_device(): lax.all_gather(linear_weight, 'dp', axis=0, tiled=True)  87 us
    reduce_scatter x1, waiting for transfers between devices, per_device(): lax.psum_scatter(in_terms.astype(jnp.bfloat16), 'mp', scatter_dimension=1...  69.3 us
    reduce_scatter x1, waiting for transfers between devices, per_device(): lax.psum_scatter(out_terms.astype(jnp.bfloat16), 'mp', scatter_dimension=...  64.7 us
    all_gather x1, waiting for transfers between devices, per_device(): features = lax.all_gather(inputs, 'mp', axis=1, tiled=True)  48.2 us
  transfers between devices with their start and end apart: 8, of which 8 were waited for; matrix products, arithmetic and copies ran while one was open for 4% of the time, Pallas kernels for 0%

commit v1 on v0

v1 whole, which is shorter than its diff:
```python
import functools

import jax
import jax.numpy as jnp
from jax import lax
from jax.experimental import pallas as pl
from jax.experimental.pallas import tpu as pltpu
from jax.sharding import PartitionSpec as P

AXES = ("dp", "mp")
ZN, YN = 8, 4
BF = jnp.bfloat16
F32 = jnp.float32
VMEM_BYTES = 60 * 1024 * 1024


def position(device):
    dp, mp = divmod(device, 16)
    return dp // 8, dp % 8, mp // 8, (mp // 2) % 4, mp % 2


def number(x, z, y, core):
    x %= 4
    return ((x // 2) * 8 + z % 8) * 16 + (x % 2) * 8 + (y % 4) * 2 + core


def permutation(target):
    pairs = []
    for device in range(256):
        h, z, l, y, c = position(device)
        to = target(2 * h + l, h, z, l, y, c)
        if to is not None:
            pairs.append((device, number(*to)))
    return pairs


def inverse(pairs):
    return [(b, a) for a, b in pairs]


Z_UP = permutation(lambda x, h, z, l, y, c: (x, z + 1, y, c))
Z_DOWN = inverse(Z_UP)
CORE = permutation(lambda x, h, z, l, y, c: (x, z, y, 1 - c))
WEIGHT = permutation(lambda x, h, z, l, y, c: (x + 1 if c == h else x - 1, z, y, h))
ACROSS = permutation(lambda x, h, z, l, y, c: (3 - x, z, y, c))
FUSE = permutation(lambda x, h, z, l, y, c: (x, z, y, 1 - c) if c != l else None)
X_STEPS = [permutation(lambda x, h, z, l, y, c, d=d: (x + d, z, y, c) if c == l else None) for d in (1, -1, 2)]
Y_STEPS = [permutation(lambda x, h, z, l, y, c, d=d: (x, z, y + d, c)) for d in (1, -1, 2)]
Z_GROUPS = [list(range(8)), list(range(8, 16))]


def move(value, pairs):
    return lax.ppermute(value, AXES, pairs)


def add(*terms):
    return functools.reduce(jnp.add, [t.astype(F32) for t in terms]).astype(BF)


ANY = pl.BlockSpec(memory_space=pl.ANY)
SMEM = pl.BlockSpec(memory_space=pltpu.SMEM)
VMEM = pl.BlockSpec(memory_space=pltpu.VMEM)
I_Z, I_Y, I_C, I_H, I_HA, I_L = range(6)


def block(j):
    return pl.ds(pl.multiple_of(j * 256, 256), 256)


def rows_of(token):
    return pl.ds(pl.multiple_of(token * 384, 384), 384)


class Copies:
    def __init__(self, sems):
        self.sems, self.used = sems, 0

    def start(self, src, dst):
        copy = pltpu.make_async_copy(src, dst, self.sems.at[self.used])
        self.used += 1
        copy.start()
        return copy


def wait(copies):
    for copy in copies:
        copy.wait()


def dot(a, b, da=1, db=0):
    return lax.dot_general(a, b, (((da,), (db,)), ((), ())), preferred_element_type=F32)


def call(kernel, outs, scratch, n_sems, args, name, out_space=VMEM, near=()):
    return pl.pallas_call(
        kernel,
        out_shape=outs,
        in_specs=[SMEM] + [VMEM if i in near else ANY for i in range(1, len(args))],
        out_specs=jax.tree.map(lambda _: out_space, outs),
        scratch_shapes=[*scratch, pltpu.SemaphoreType.DMA((n_sems,))],
        compiler_params=pltpu.CompilerParams(vmem_limit_bytes=VMEM_BYTES),
        cost_estimate=pl.CostEstimate(flops=1000, bytes_accessed=1000, transcendentals=0),
        name=name,
    )(*args)


def shape(*dims, dtype=BF):
    return jax.ShapeDtypeStruct(dims, dtype)


STEPS = (0, 3, 1, 2)


def column(idx, step, slot):
    core = idx[I_C] if slot % 2 == 0 else 1 - idx[I_C]
    return 2 * lax.rem(idx[I_Y] + step, YN) + core


def token_of(idx, slot):
    return idx[I_HA] if slot < 2 else 1 - idx[I_HA]


def projection_kernel(idx, *refs):
    pieces, w = refs[:4], refs[4]
    far, own, xs, ws, sems = refs[5:]
    copies = Copies(sems)
    c = idx[I_C]
    features = []
    for place, token in enumerate((1 - c, c)):
        pair = jnp.where(token == idx[I_HA], 0, 2)
        for piece, step in zip(pieces, STEPS):
            for slot in range(2):
                features.append(copies.start(piece.at[pair + slot], xs.at[place, :, block(column(idx, step, slot))]))
        if place == 0:
            weights = [copies.start(w.at[:, pl.ds(256 * p, 256)], ws.at[p]) for p in range(3)]
    for place, out in enumerate((far, own)):
        wait(features[8 * place : 8 * place + 8])
        for p in range(3):
            if place == 0:
                weights[p].wait()
            out[:, 256 * p : 256 * p + 256] = dot(xs[place], ws[p].reshape(2048, 256))


def projections(idx, x, w):
    scratch = [pltpu.VMEM((2, 384, 2048), BF), pltpu.VMEM((3, 8, 256, 256), BF)]
    return call(projection_kernel, [shape(384, 768, dtype=F32)] * 2, scratch, 19, (idx, *x, w), "projections")


def output_weight_copies(copies, w, dst):
    return [copies.start(w.at[j, pl.ds(768, 384)], dst.at[:, 256 * j : 256 * j + 256]) for j in range(ZN)]


def cot_copies(copies, idx, local, remote, dst):
    c, h = idx[I_C], idx[I_H]
    half = pl.ds(pl.multiple_of(c * 2048, 2048), 2048)
    return [copies.start(local.at[:, half], dst.at[rows_of(h)]), copies.start(remote, dst.at[rows_of(1 - h)])]


def hidden_cot_kernel(idx, local, remote, w, other, own, ds, os, sems):
    copies = Copies(sems)
    wait(cot_copies(copies, idx, local, remote, ds) + output_weight_copies(copies, w, os))
    c = idx[I_C]
    other[...] = dot(ds[rows_of(1 - c)], os[...], 1, 1)
    own[...] = dot(ds[rows_of(c)], os[...], 1, 1)


def hidden_cots(idx, local, remote, w):
    outs = [shape(384, 384, dtype=F32)] * 2
    scratch = [pltpu.VMEM((768, 2048), BF), pltpu.VMEM((384, 2048), BF)]
    return call(hidden_cot_kernel, outs, scratch, 10, (idx, local, remote, w), "hidden_cots")


def activation_kernel(own, far, hidden, activated, slope):
    gate = own[:, :384] + far[:, :384]
    linear = own[:, 384:] + far[:, 384:]
    k = 0.7978845608028654
    t = jnp.tanh(k * (gate + 0.044715 * gate * gate * gate))
    half = 0.5 * (1.0 + t)
    value = gate * half
    activated[...] = value
    hidden[...] = (value * linear).astype(BF)
    slope[...] = linear * (half + 0.5 * gate * (1.0 - t * t) * (k * (1.0 + 3 * 0.044715 * gate * gate)))


def activation(own, far):
    return pl.pallas_call(
        activation_kernel,
        out_shape=[shape(384, 384), shape(384, 384, dtype=F32), shape(384, 384, dtype=F32)],
        cost_estimate=pl.CostEstimate(flops=1000, bytes_accessed=1000, transcendentals=0),
        name="activation",
    )(own, far)


def cot_kernel(own, far, activated, slope, cots):
    cot = own[...] + far[...]
    cots[:, :384] = (cot * slope[...]).astype(BF)
    cots[:, 384:] = (cot * activated[...]).astype(BF)


def cotangents(own, far, activated, slope):
    return pl.pallas_call(
        cot_kernel,
        out_shape=shape(384, 768),
        cost_estimate=pl.CostEstimate(flops=1000, bytes_accessed=1000, transcendentals=0),
        name="cotangents",
    )(own, far, activated, slope)


def stack_tokens(idx, own, other, dst):
    dst[rows_of(idx[I_C])] = own[...]
    dst[rows_of(1 - idx[I_C])] = other[...]


def transposed(idx, own, other, dst):
    dst[:, rows_of(idx[I_C])] = own[...].T
    dst[:, rows_of(1 - idx[I_C])] = other[...].T


def weight_grad_kernel(idx, hidden, hidden_far, cots, cots_far, local, remote, *refs):
    pieces = refs[:4]
    out, ht, ct, ds, xs, stage, sems = refs[4:]
    copies = Copies(sems)
    out_cots = cot_copies(copies, idx, local, remote, ds)
    arriving = []
    for piece, step in zip(pieces, STEPS):
        for core in range(2):
            j = column(idx, step, core)
            both = [copies.start(piece.at[slot], xs.at[rows_of(token_of(idx, slot)), block(j)]) for slot in (core, 2 + core)]
            arriving.append((j, both))
    transposed(idx, hidden, hidden_far, ht)
    transposed(idx, cots, cots_far, ct)
    wait(out_cots)
    for j in range(ZN):
        stage[j, 768:] = dot(ht[...], ds[:, 256 * j : 256 * j + 256]).astype(BF)
    leaving = []
    for j, both in arriving:
        wait(both)
        stage[j, :768] = dot(ct[...], xs[:, block(j)]).astype(BF)
        leaving.append(copies.start(stage.at[j], out.at[j]))
    wait(leaving)


def weight_grads(idx, hidden, hidden_far, cots, cots_far, local, remote, x):
    half = pltpu.VMEM((768, 2048), BF)
    scratch = [pltpu.VMEM((384, 768), BF), pltpu.VMEM((768, 768), BF), half, half, pltpu.VMEM((8, 1152, 256), BF)]
    args = (idx, hidden, hidden_far, cots, cots_far, local, remote, *x)
    return call(weight_grad_kernel, shape(8, 1152, 256), scratch, 26, args, "weight_grads", ANY, (1, 2, 3, 4))


def output_kernel(idx, own, other, w, here, up, down, across_up, across_down, hs, os, sems):
    copies = Copies(sems)
    weights = output_weight_copies(copies, w, os)
    stack_tokens(idx, own, other, hs)
    wait(weights)
    for step, out in ((0, here), (1, up), (3, down), (2, None)):
        for slot in range(4):
            value = dot(hs[rows_of(token_of(idx, slot))], os[:, block(column(idx, step, slot))]).astype(BF)
            if out is not None:
                out[slot] = value
            else:
                (across_up, across_down)[slot // 2][slot % 2] = value


def outputs(idx, own, other, w):
    outs = [shape(4, 384, 256)] * 3 + [shape(2, 384, 256)] * 2
    scratch = [pltpu.VMEM((768, 384), BF), pltpu.VMEM((384, 2048), BF)]
    return call(output_kernel, outs, scratch, 8, (idx, own, other, w), "outputs", near=(1, 2))


def input_grad_kernel(idx, own, other, w, first, second, cs, ws, sf, ss, sems):
    copies = Copies(sems)
    weights = [copies.start(w.at[:, pl.ds(256 * p, 256)], ws.at[:, :, 256 * p : 256 * p + 256]) for p in range(3)]
    stack_tokens(idx, own, other, cs)
    wait(weights)
    leaving = []
    for step in range(YN):
        for core in range(2):
            j = column(idx, step, core)
            for pair, (stage, out) in enumerate(((sf, first), (ss, second))):
                stage[core, step] = dot(cs[rows_of(token_of(idx, 2 * pair))], ws[j], 1, 1).astype(BF)
                leaving.append(copies.start(stage.at[core, step], out.at[core, step]))
    wait(leaving)


def input_grads(idx, own, other, w):
    stage = pltpu.VMEM((2, 4, 384, 256), BF)
    scratch = [pltpu.VMEM((768, 768), BF), pltpu.VMEM((8, 256, 768), BF), stage, stage]
    return call(input_grad_kernel, [shape(2, 4, 384, 256)] * 2, scratch, 19, (idx, own, other, w), "input_grads", ANY, (1, 2))


def pack_kernel(gate, linear, out, packed):
    packed[0:256] = gate[:, 0:256]
    packed[256:512, 0:128] = gate[:, 256:384]
    packed[256:512, 128:256] = linear[:, 0:128]
    packed[512:768] = linear[:, 128:384]
    packed[768:1152] = out[...]


def pack(gate, linear, out):
    return pl.pallas_call(pack_kernel, out_shape=shape(1152, 256), name="pack")(gate, linear, out)


def finish_kernel(share, gate, linear, out):
    gate[...] = share[:384].astype(F32).T
    linear[...] = share[384:768].astype(F32).T
    out[...] = share[768:].astype(F32)


def finish(share):
    outs = [shape(256, 384, dtype=F32), shape(256, 384, dtype=F32), shape(384, 256, dtype=F32)]
    cost = pl.CostEstimate(flops=0, bytes_accessed=50_000_000, transcendentals=0)
    return pl.pallas_call(finish_kernel, out_shape=outs, cost_estimate=cost, name="finish")(share)


def sum_x(first, second):
    from_above = move(first, inverse(X_STEPS[0]))
    from_below = move(second, inverse(X_STEPS[1]))
    from_across = move(second, X_STEPS[2])
    return add(first, from_above, from_below, from_across)


def split(total, is_l):
    return jnp.where(is_l, total[0], move(total[1], inverse(FUSE)))


def per_device(inputs, out_cotangent, gate_weight, linear_weight, output_weight):
    dp, mp = lax.axis_index("dp"), lax.axis_index("mp")
    h, z, l, y, c = dp // 8, dp % 8, mp // 8, (mp // 2) % 4, mp % 2
    is_l = c == l
    ha = jnp.where(is_l | (l == 1), h, 1 - h)
    idx = jnp.stack([z, y, c, h, ha, l]).astype(jnp.int32)

    shard = move(pack(gate_weight, linear_weight, output_weight), WEIGHT)
    mine = jnp.stack([inputs, move(inputs, FUSE)])
    shard, mine = lax.optimization_barrier((shard, mine))
    w = lax.all_gather(shard, "dp", axis_index_groups=Z_GROUPS)
    below, above, across = [move(mine, pairs) for pairs in X_STEPS]
    half = lax.dynamic_slice(out_cotangent, (0, c * 2048), (384, 2048))
    slots = jnp.concatenate([jnp.where(is_l, mine, below), jnp.where(is_l, across, above)])
    slots, half = lax.optimization_barrier((slots, half))
    x = [slots, *[move(slots, pairs) for pairs in Y_STEPS]]
    remote = move(half, ACROSS)

    far, own = projections(idx, x, w)
    idx, far = lax.optimization_barrier((idx, far))
    far = move(far, CORE)
    hc_far, hc_own = hidden_cots(idx, out_cotangent, remote, w)
    hc_far = move(hc_far, CORE)
    hidden, activated, slope = activation(own, far)
    hidden_far = move(hidden, CORE)
    hc_far, activated = lax.optimization_barrier((hc_far, activated))
    cots = cotangents(hc_own, hc_far, activated, slope)
    cots_far = move(cots, CORE)

    hidden_far, cots = lax.optimization_barrier((hidden_far, cots))
    here, up, down, across_up, across_down = outputs(idx, hidden, hidden_far, w)
    idx, across_up, across_down = lax.optimization_barrier((idx, across_up, across_down))
    parts = weight_grads(idx, hidden, hidden_far, cots, cots_far, out_cotangent, remote, x)
    idx, parts = lax.optimization_barrier((idx, parts))
    share = lax.psum_scatter(parts.reshape(8 * 1152, 256), "dp", scatter_dimension=0, axis_index_groups=Z_GROUPS, tiled=True)
    first, second = input_grads(idx, cots, cots_far, w)

    zero = jnp.zeros((), BF)
    up = add(up, lax.pad(move(across_up, Y_STEPS[0]), zero, ((0, 2, 0), (0, 0, 0), (0, 0, 0))))
    down = add(down, lax.pad(move(across_down, Y_STEPS[1]), zero, ((2, 0, 0), (0, 0, 0), (0, 0, 0))))
    sums = add(here, move(up, Y_STEPS[0]), move(down, Y_STEPS[1]))

    layer_output = split(sum_x(sums[:2], sums[2:]), is_l)

    total = sum_x(first, second)
    total, share = lax.optimization_barrier((total, share))
    gate_grad, linear_grad, output_grad = finish(move(share, inverse(WEIGHT)))
    rows = split(total, is_l)
    input_grad = add(rows[0], move(rows[1], Y_STEPS[0]), move(rows[3], Y_STEPS[1]), move(rows[2], Y_STEPS[2]))
    return (layer_output, input_grad, gate_grad, linear_grad, output_grad)


def solution(mesh):
    return jax.shard_map(
        per_device,
        mesh=mesh,
        in_specs=(P("dp", "mp"), P("dp", None), P("dp", "mp"), P("dp", "mp"), P("mp", "dp")),
        out_specs=(P("dp", "mp"), P("dp", "mp"), P("dp", "mp"), P("dp", "mp"), P("mp", "dp")),
        check_vma=False,
    )
```

time: 922 us -> 217 us (0.24)
  waiting for transfers between devices: 858 us -> 91.8 us
  Pallas kernels: 0 us -> 48.2 us
  starting transfers between devices: 0.5 us -> 45.9 us
  matrix products: 40.7 us -> 0 us
    reduce_scatter x4 -> x1, waiting for transfers between devices: 539 us -> 4.36 us  [per_device(): lax.psum_scatter(parts.reshape(8 * 1152, 256), 'dp', scatter_dimension=0,...]
    all_gather x4 -> x1, waiting for transfers between devices: 316 us -> 9.71 us  [per_device(): w = lax.all_gather(shard, 'dp', axis_index_groups=Z_GROUPS)]
    ppermute x0 -> x29, waiting for transfers between devices: none -> 77.7 us  [move(): return lax.ppermute(value, AXES, pairs)]
    pallas_call x0 -> x9, Pallas kernels: none -> 48.2 us  [the longest x5 38.5 us: call(): pl.pallas_call(kernel, out_shape=outs, in_specs=[SMEM] + [VMEM if i in ne...]
    ppermute x0 -> x29, starting transfers between devices: none -> 45.9 us  [move(): return lax.ppermute(value, AXES, pairs)]
    dot_general x8 -> x0, matrix products: 40.7 us -> none  [the longest x1 8.17 us: per_device(): lax.dot_general(features, both_cot, contract, preferred_element_type=jnp....]
  transfers between devices with their start and end apart: 8 -> 31, of which waited for: 8 -> 15; matrix products, arithmetic and copies ran while one was open for 4% -> 4% of each run, Pallas kernels for 0% -> 14%
where the time goes in v1:
time: 217 us
  waiting for transfers between devices  91.8 us (42%)
  Pallas kernels  48.2 us (22%)
  starting transfers between devices  45.9 us (21%)
  between operations  14.4 us (7%)
  local copies, waits for them, and re-layouts  10.8 us (5%)
  other arithmetic  5.45 us (3%)
    ppermute x29, waiting for transfers between devices, move(): return lax.ppermute(value, AXES, pairs)  77.7 us
    ppermute x29, starting transfers between devices, move(): return lax.ppermute(value, AXES, pairs)  45.9 us
    pallas_call x5, Pallas kernels, call(): pl.pallas_call(kernel, out_shape=outs, in_specs=[SMEM] + [VMEM if i in ne...  38.5 us
    all_gather x1, waiting for transfers between devices, per_device(): w = lax.all_gather(shard, 'dp', axis_index_groups=Z_GROUPS)  9.71 us
    unnamed x34, local copies, waits for them, and re-layouts  7.22 us
    reduce_scatter x1, waiting for transfers between devices, per_device(): lax.psum_scatter(parts.reshape(8 * 1152, 256), 'dp', scatter_dimension=0,...  4.36 us
  transfers between devices with their start and end apart: 31, of which 15 were waited for; matrix products, arithmetic and copies ran while one was open for 4% of the time, Pallas kernels for 14%

profile of v1, /device:TPU:1, one launch (start us, length us, event | category | flops | bytes accessed | tf_op | source)
XLA Modules:
  0.0 216.6 jit_solution(4096720865020571272)
XLA Ops:
  9.2 3.9 %collective-permute-start = (bf16[1152,256]{1,0:T(8,128)(2,1)}, bf16[1152,256]{1,0:T(8,128)(2,1)S(1)}, u32[]{:S(2)}, u32[]{:S(2)}) collective-permute-start(bf16[1152,256]{1,0:T(8,128)(2,1)} %pack.1), channel_id=1, source_target_pairs={{0,8},{1,136},{2,10},{3,138},{4,12},{5,140},{6,14},{7,142},{8,128}... | collective-permute-start | bytes 1769480 | tf_op jit(solution)/shard_map/ppermute | solution.py:53
  16.6 3.6 %collective-permute-done = bf16[1152,256]{1,0:T(8,128)(2,1)S(1)} collective-permute-done((bf16[1152,256]{1,0:T(8,128)(2,1)}, bf16[1152,256]{1,0:T(8,128)(2,1)S(1)}, u32[]{:S(2)}, u32[]{:S(2)}) %collective-permute-start) | collective-permute-done | bytes 589856 | tf_op jit(solution)/shard_map/ppermute | solution.py:53
  24.4 2.8 %constant_dynamic-slice_fusion = bf16[384,2048]{1,0:T(8,128)(2,1)} fusion(bf16[384,4096]{1,0:T(8,128)(2,1)} %local.3, s32[]{:T(128)S(6)} %select_n.70), kind=kLoop, calls=%fused_computation.22 | loop fusion | bytes 3145732 | tf_op jit(solution)/shard_map/dynamic_slice | solution.py:338
  27.2 3.6 %collective-permute-done.2 = bf16[2,384,256]{2,1,0:T(8,128)(2,1)S(1)} collective-permute-done((bf16[2,384,256]{2,1,0:T(8,128)(2,1)S(1)}, bf16[2,384,256]{2,1,0:T(8,128)(2,1)S(1)}, u32[]{:S(2)}, u32[]{:S(2)}) %collective-permute-start.2) | collective-permute-done | bytes 393248 | tf_op jit(solution)/shard_map/ppermute | solution.py:53
  30.9 7.0 %collective-permute-done.4 = bf16[2,384,256]{2,1,0:T(8,128)(2,1)S(1)} collective-permute-done((bf16[2,384,256]{2,1,0:T(8,128)(2,1)S(1)}, bf16[2,384,256]{2,1,0:T(8,128)(2,1)S(1)}, u32[]{:S(2)}, u32[]{:S(2)}) %collective-permute-start.4) | collective-permute-done | bytes 393248 | tf_op jit(solution)/shard_map/ppermute | solution.py:53
  43.6 12.9 %collective-permute-done.5.refs_1_ = bf16[4,384,256]{2,1,0:T(8,128)(2,1)S(1)} collective-permute-done((bf16[4,384,256]{2,1,0:T(8,128)(2,1)S(1)}, bf16[4,384,256]{2,1,0:T(8,128)(2,1)S(1)}, u32[]{:S(2)}, u32[]{:S(2)}) %collective-permute-start.5) | collective-permute-done | bytes 786464 | tf_op jit(solution)/shard_map/ppermute | solution.py:53
  56.5 18.0 %collective-permute-done.7.refs_3_ = bf16[4,384,256]{2,1,0:T(8,128)(2,1)} collective-permute-done((bf16[4,384,256]{2,1,0:T(8,128)(2,1)S(1)}, bf16[4,384,256]{2,1,0:T(8,128)(2,1)}, u32[]{:S(2)}, u32[]{:S(2)}) %collective-permute-start.7) | collective-permute-done | bytes 786464 | tf_op jit(solution)/shard_map/ppermute | solution.py:53
  74.5 9.7 %all-gather.3.cloned.1.call-done = bf16[9216,256]{1,0:T(8,128)(2,1)} async-done(((bf16[1152,256]{1,0:T(8,128)(2,1)}), bf16[9216,256]{1,0:T(8,128)(2,1)}) %all-gather.3.cloned.1.call-update) | async-done | bytes 4718608 | tf_op jit(solution)/shard_map/all_gather | solution.py:336
  84.2 8.4 %projections.1 = (f32[384,768]{1,0:T(8,128)}, f32[384,768]{1,0:T(8,128)}) custom-call(s32[6]{0:T(128)} %stack.36.idx, bf16[4,384,256]{2,1,0:T(8,128)(2,1)} %copy-done, bf16[4,384,256]{2,1,0:T(8,128)(2,1)} %copy-done.2, bf16[4,384,256]{2,1,0:T(8,128)(2,1)} %collective-permute-done.6.refs_2_, bf16[4,384,256]{2,1,0:T(8,128)(2,1)} %collective-permute-done.7.refs_3_, ...), custom_call_target="tpu_custom_call" | custom-call | flops 1000 | bytes 1000 | tf_op jit(solution)/shard_map/projections/pallas_call | solution.py:95
  94.5 5.7 %hidden_cots.1 = (f32[384,384]{1,0:T(8,128)}, f32[384,384]{1,0:T(8,128)}) custom-call(s32[6]{0:T(128)} %stack.36.idx, bf16[384,4096]{1,0:T(8,128)(2,1)} %local.3, bf16[384,2048]{1,0:T(8,128)(2,1)} %copy-done.1, bf16[8,1152,256]{2,1,0:T(8,128)(2,1)} %bitcast.32), custom_call_target="tpu_custom_call" | custom-call | flops 1000 | bytes 1000 | tf_op jit(solution)/shard_map/hidden_cots/pallas_call | solution.py:95
  101.3 3.0 %activation.1 = (bf16[384,384]{1,0:T(8,128)(2,1)}, f32[384,384]{1,0:T(8,128)}, f32[384,384]{1,0:T(8,128)}) custom-call(f32[384,768]{1,0:T(8,128)} %get-tuple-element.44.own, f32[384,768]{1,0:T(8,128)} %copy-done.5), custom_call_target="tpu_custom_call" | custom-call | flops 1000 | bytes 1000 | tf_op jit(solution)/shard_map/activation/pallas_call | solution.py:186
  105.2 2.5 %cotangents.1.cots.own = bf16[384,768]{1,0:T(8,128)(2,1)} custom-call(f32[384,384]{1,0:T(8,128)} %get-tuple-element.48.own, f32[384,384]{1,0:T(8,128)} %copy-done.13, f32[384,384]{1,0:T(8,128)} %get-tuple-element.52.activated, f32[384,384]{1,0:T(8,128)} %get-tuple-element.53.slope), custom_call_target="tpu_custom_call" | custom-call | flops 1000 | bytes 1000 | tf_op jit(solution)/shard_map/cotangents/pallas_call | solution.py:201
  111.0 5.5 %outputs.1 = (bf16[4,384,256]{2,1,0:T(8,128)(2,1)}, bf16[4,384,256]{2,1,0:T(8,128)(2,1)}, bf16[4,384,256]{2,1,0:T(8,128)(2,1)}, bf16[2,384,256]{2,1,0:T(8,128)(2,1)}, bf16[2,384,256]{2,1,0:T(8,128)(2,1)}) custom-call(s32[6]{0:T(128)} %stack.36.idx, bf16[384,384]{1,0:T(8,128)(2,1)} %get-tuple-element.46.own.hidden, bf16[384,384]{1,0:T(8,128)(2,1)} %copy-done.7, ...), custom_call_target="tpu_custom_call" | custom-call | flops 1000 | bytes 1000 | tf_op jit(solution)/shard_map/outputs/pallas_call | solution.py:95
  117.3 12.3 %weight_grads.1 = bf16[8,1152,256]{2,1,0:T(8,128)(2,1)} custom-call(s32[6]{0:T(128)} %stack.36.idx, bf16[384,384]{1,0:T(8,128)(2,1)} %get-tuple-element.46.own.hidden, bf16[384,384]{1,0:T(8,128)(2,1)} %copy-done.7, bf16[384,768]{1,0:T(8,128)(2,1)} %cotangents.1.cots.own, bf16[384,768]{1,0:T(8,128)(2,1)} %copy-done.3, bf16[384,4096]{1,0:T(8,128)(2,1)} %local.3, ...), custom_call_target="tpu_custom_call" | custom-call | flops 1000 | bytes 1000 | tf_op jit(solution)/shard_map/weight_grads/pallas_call | solution.py:95
  130.6 2.4 %collective-permute-start.14 = (bf16[2,384,256]{2,1,0:T(8,128)(2,1)S(1)}, bf16[2,384,256]{2,1,0:T(8,128)(2,1)S(1)}, u32[]{:S(2)}, u32[]{:S(2)}) collective-permute-start(bf16[2,384,256]{2,1,0:T(8,128)(2,1)S(1)} %copy-done.16), channel_id=1, source_target_pairs={{0,6},{1,7},{2,0},{3,1},{4,2},{5,3},{6,4},{7,5},{8,14},{9,15},{10,... | collective-permute-start | bytes 1179656 | tf_op jit(solution)/shard_map/ppermute | solution.py:53
  133.0 6.7 %input_grads.1 = (bf16[2,4,384,256]{3,2,1,0:T(8,128)(2,1)}, bf16[2,4,384,256]{3,2,1,0:T(8,128)(2,1)}) custom-call(s32[6]{0:T(128)} %stack.36.idx, bf16[384,768]{1,0:T(8,128)(2,1)} %cotangents.1.cots.own, bf16[384,768]{1,0:T(8,128)(2,1)} %copy-done.3, bf16[8,1152,256]{2,1,0:T(8,128)(2,1)} %bitcast.34), custom_call_target="tpu_custom_call" | custom-call | flops 1000 | bytes 1000 | tf_op jit(solution)/shard_map/input_grads/pallas_call | solution.py:95
  140.6 6.1 %collective-permute-start.22 = (bf16[2,4,384,256]{3,2,1,0:T(8,128)(2,1)}, bf16[2,4,384,256]{3,2,1,0:T(8,128)(2,1)S(1)}, u32[]{:S(2)}, u32[]{:S(2)}) collective-permute-start(bf16[2,4,384,256]{3,2,1,0:T(8,128)(2,1)} %get-tuple-element.66), channel_id=1, source_target_pairs={{136,0},{138,2},{140,4},{142,6},{1,9},{3,11},{5,13},{7,15},{152,16... | collective-permute-start | bytes 4718600 | tf_op jit(solution)/shard_map/ppermute | solution.py:53
  148.8 2.7 %collective-permute-start.15 = (bf16[4,384,256]{2,1,0:T(8,128)(2,1)S(1)}, bf16[4,384,256]{2,1,0:T(8,128)(2,1)S(1)}, u32[]{:S(2)}, u32[]{:S(2)}) collective-permute-start(bf16[4,384,256]{2,1,0:T(8,128)(2,1)S(1)} %add_convert_fusion.2), channel_id=1, source_target_pairs={{0,6},{1,7},{2,0},{3,1},{4,2},{5,3},{6,4},{7,5},{8,14},{9,15},{10,... | collective-permute-start | bytes 2359304 | tf_op jit(solution)/shard_map/ppermute | solution.py:53
  152.0 16.9 %collective-permute-done.15 = bf16[4,384,256]{2,1,0:T(8,128)(2,1)S(1)} collective-permute-done((bf16[4,384,256]{2,1,0:T(8,128)(2,1)S(1)}, bf16[4,384,256]{2,1,0:T(8,128)(2,1)S(1)}, u32[]{:S(2)}, u32[]{:S(2)}) %collective-permute-start.15) | collective-permute-done | bytes 786464 | tf_op jit(solution)/shard_map/ppermute | solution.py:53
  168.8 3.7 %collective-permute-done.13 = bf16[4,384,256]{2,1,0:T(8,128)(2,1)S(1)} collective-permute-done((bf16[4,384,256]{2,1,0:T(8,128)(2,1)S(1)}, bf16[4,384,256]{2,1,0:T(8,128)(2,1)S(1)}, u32[]{:S(2)}, u32[]{:S(2)}) %collective-permute-start.13) | collective-permute-done | bytes 786464 | tf_op jit(solution)/shard_map/ppermute | solution.py:53
  178.9 2.3 %collective-permute-done.22 = bf16[2,4,384,256]{3,2,1,0:T(8,128)(2,1)S(1)} collective-permute-done((bf16[2,4,384,256]{3,2,1,0:T(8,128)(2,1)}, bf16[2,4,384,256]{3,2,1,0:T(8,128)(2,1)S(1)}, u32[]{:S(2)}, u32[]{:S(2)}) %collective-permute-start.22) | collective-permute-done | bytes 1572896 | tf_op jit(solution)/shard_map/ppermute | solution.py:53
  184.0 4.4 %reduce-scatter.2.cloned.1.call-done = bf16[1152,256]{1,0:T(8,128)(2,1)} async-done(((bf16[9216,256]{1,0:T(8,128)(2,1)}), bf16[1152,256]{1,0:T(8,128)(2,1)}) %reduce-scatter.2.cloned.1.call-update) | async-done | bytes 589840 | tf_op jit(solution)/shard_map/reduce_scatter | solution.py:360
  192.7 3.8 %collective-permute-start.28 = (bf16[1152,256]{1,0:T(8,128)(2,1)S(1)}, bf16[1152,256]{1,0:T(8,128)(2,1)S(1)}, u32[]{:S(2)}, u32[]{:S(2)}) collective-permute-start(bf16[1152,256]{1,0:T(8,128)(2,1)S(1)} %copy-done.14), channel_id=1, source_target_pairs={{8,0},{136,1},{10,2},{138,3},{12,4},{140,5},{14,6},{142,7},{128,8}... | collective-permute-start | bytes 1769480 | tf_op jit(solution)/shard_map/ppermute | solution.py:53
  196.6 2.8 %collective-permute-start.27 = (bf16[384,256]{1,0:T(8,128)(2,1)S(1)}, bf16[384,256]{1,0:T(8,128)(2,1)S(1)}, u32[]{:S(2)}, u32[]{:S(2)}) collective-permute-start(bf16[384,256]{1,0:T(8,128)(2,1)S(1)} %get-tuple-element.74), channel_id=1, source_target_pairs={{0,4},{1,5},{2,6},{3,7},{4,0},{5,1},{6,2},{7,3},{8,12},{9,13},{10,... | collective-permute-start | bytes 589832 | tf_op jit(solution)/shard_map/ppermute | solution.py:53
  (101 shorter events, 51.5 us)
Async XLA Ops:
  7.2 77.0 %all-gather.3.cloned.1.call-start = ((), (), s32[]{:S(2)}) async-start(), calls=%async_computation.2 | async-start | bytes 5308416 | tf_op jit(solution)/shard_map/all_gather | solution.py:336
  9.2 11.0 %collective-permute-start = (bf16[1152,256]{1,0:T(8,128)(2,1)}, bf16[1152,256]{1,0:T(8,128)(2,1)S(1)}, u32[]{:S(2)}, u32[]{:S(2)}) collective-permute-start(bf16[1152,256]{1,0:T(8,128)(2,1)} %pack.1), channel_id=1, source_target_pairs={{0,8},{1,136},{2,10},{3,138},{4,12},{5,140},{6,14},{7,142},{8,128}... | collective-permute-start | bytes 1769480 | tf_op jit(solution)/shard_map/ppermute | solution.py:53
  21.1 167.3 %reduce-scatter.2.cloned.1.call-start = ((), (), s32[]{:S(2)}) async-start(), calls=%async_computation.1 | async-start | bytes 5308416 | tf_op jit(solution)/shard_map/reduce_scatter | solution.py:360
  21.1 9.7 %collective-permute-start.2 = (bf16[2,384,256]{2,1,0:T(8,128)(2,1)S(1)}, bf16[2,384,256]{2,1,0:T(8,128)(2,1)S(1)}, u32[]{:S(2)}, u32[]{:S(2)}) collective-permute-start(bf16[2,384,256]{2,1,0:T(8,128)(2,1)S(1)} %pad_maximum_fusion.1), channel_id=1, source_target_pairs={{0,8},{2,10},{4,12},{6,14},{9,129},{11,131},{13,133},{15,135},{16,... | collective-permute-start | bytes 1179656 | tf_op jit(solution)/shard_map/ppermute | solution.py:53
  23.1 14.8 %collective-permute-start.4 = (bf16[2,384,256]{2,1,0:T(8,128)(2,1)S(1)}, bf16[2,384,256]{2,1,0:T(8,128)(2,1)S(1)}, u32[]{:S(2)}, u32[]{:S(2)}) collective-permute-start(bf16[2,384,256]{2,1,0:T(8,128)(2,1)S(1)} %pad_maximum_fusion.1), channel_id=1, source_target_pairs={{0,136},{2,138},{4,140},{6,142},{9,1},{11,3},{13,5},{15,7},{16,152... | collective-permute-start | bytes 1179656 | tf_op jit(solution)/shard_map/ppermute | solution.py:53
  38.0 55.3 %collective-permute-start.10 = (bf16[384,2048]{1,0:T(8,128)(2,1)}, bf16[384,2048]{1,0:T(8,128)(2,1)S(1)}, u32[]{:S(2)}, u32[]{:S(2)}) collective-permute-start(bf16[384,2048]{1,0:T(8,128)(2,1)} %constant_dynamic-slice_fusion), channel_id=1, source_target_pairs={{0,136},{1,137},{2,138},{3,139},{4,140},{5,141},{6,142},{7,143},{8... | collective-permute-start | bytes 4718600 | tf_op jit(solution)/shard_map/ppermute | solution.py:53
  38.6 17.9 %collective-permute-start.5 = (bf16[4,384,256]{2,1,0:T(8,128)(2,1)S(1)}, bf16[4,384,256]{2,1,0:T(8,128)(2,1)S(1)}, u32[]{:S(2)}, u32[]{:S(2)}) collective-permute-start(bf16[4,384,256]{2,1,0:T(8,128)(2,1)S(1)} %pad_maximum_fusion.refs_0_), channel_id=1, source_target_pairs={{0,2},{1,3},{2,4},{3,5},{4,6},{5,7},{6,0},{7,1},{8,10},{9,11},{10,... | collective-permute-start | bytes 2359304 | tf_op jit(solution)/shard_map/ppermute | solution.py:53
  39.9 16.6 %collective-permute-start.6 = (bf16[4,384,256]{2,1,0:T(8,128)(2,1)S(1)}, bf16[4,384,256]{2,1,0:T(8,128)(2,1)}, u32[]{:S(2)}, u32[]{:S(2)}) collective-permute-start(bf16[4,384,256]{2,1,0:T(8,128)(2,1)S(1)} %pad_maximum_fusion.refs_0_), channel_id=1, source_target_pairs={{0,6},{1,7},{2,0},{3,1},{4,2},{5,3},{6,4},{7,5},{8,14},{9,15},{10,... | collective-permute-start | bytes 2359304 | tf_op jit(solution)/shard_map/ppermute | solution.py:53
  41.4 33.1 %collective-permute-start.7 = (bf16[4,384,256]{2,1,0:T(8,128)(2,1)S(1)}, bf16[4,384,256]{2,1,0:T(8,128)(2,1)}, u32[]{:S(2)}, u32[]{:S(2)}) collective-permute-start(bf16[4,384,256]{2,1,0:T(8,128)(2,1)S(1)} %pad_maximum_fusion.refs_0_), channel_id=1, source_target_pairs={{0,4},{1,5},{2,6},{3,7},{4,0},{5,1},{6,2},{7,3},{8,12},{9,13},{10,... | collective-permute-start | bytes 2359304 | tf_op jit(solution)/shard_map/ppermute | solution.py:53
  107.7 8.8 %collective-permute-start.20 = (bf16[384,768]{1,0:T(8,128)(2,1)}, bf16[384,768]{1,0:T(8,128)(2,1)S(1)}, u32[]{:S(2)}, u32[]{:S(2)}) collective-permute-start(bf16[384,768]{1,0:T(8,128)(2,1)} %cotangents.1.cots.own), channel_id=1, source_target_pairs={{0,1},{1,0},{2,3},{3,2},{4,5},{5,4},{6,7},{7,6},{8,9},{9,8},{10,11... | collective-permute-start | bytes 1769480 | tf_op jit(solution)/shard_map/ppermute | solution.py:53
  130.6 18.1 %collective-permute-start.14 = (bf16[2,384,256]{2,1,0:T(8,128)(2,1)S(1)}, bf16[2,384,256]{2,1,0:T(8,128)(2,1)S(1)}, u32[]{:S(2)}, u32[]{:S(2)}) collective-permute-start(bf16[2,384,256]{2,1,0:T(8,128)(2,1)S(1)} %copy-done.16), channel_id=1, source_target_pairs={{0,6},{1,7},{2,0},{3,1},{4,2},{5,3},{6,4},{7,5},{8,14},{9,15},{10,... | collective-permute-start | bytes 1179656 | tf_op jit(solution)/shard_map/ppermute | solution.py:53
  133.0 18.5 %collective-permute-start.12 = (bf16[2,384,256]{2,1,0:T(8,128)(2,1)S(1)}, bf16[2,384,256]{2,1,0:T(8,128)(2,1)S(1)}, u32[]{:S(2)}, u32[]{:S(2)}) collective-permute-start(bf16[2,384,256]{2,1,0:T(8,128)(2,1)S(1)} %copy-done.15), channel_id=1, source_target_pairs={{0,2},{1,3},{2,4},{3,5},{4,6},{5,7},{6,0},{7,1},{8,10},{9,11},{10,... | collective-permute-start | bytes 1179656 | tf_op jit(solution)/shard_map/ppermute | solution.py:53
  139.7 36.9 %collective-permute-start.23 = (bf16[2,4,384,256]{3,2,1,0:T(8,128)(2,1)}, bf16[2,4,384,256]{3,2,1,0:T(8,128)(2,1)S(1)}, u32[]{:S(2)}, u32[]{:S(2)}) collective-permute-start(bf16[2,4,384,256]{3,2,1,0:T(8,128)(2,1)} %get-tuple-element.66), channel_id=1, source_target_pairs={{0,128},{2,130},{4,132},{6,134},{9,137},{11,139},{13,141},{15,143}... | collective-permute-start | bytes 4718600 | tf_op jit(solution)/shard_map/ppermute | solution.py:53
  140.6 40.6 %collective-permute-start.22 = (bf16[2,4,384,256]{3,2,1,0:T(8,128)(2,1)}, bf16[2,4,384,256]{3,2,1,0:T(8,128)(2,1)S(1)}, u32[]{:S(2)}, u32[]{:S(2)}) collective-permute-start(bf16[2,4,384,256]{3,2,1,0:T(8,128)(2,1)} %get-tuple-element.66), channel_id=1, source_target_pairs={{136,0},{138,2},{140,4},{142,6},{1,9},{3,11},{5,13},{7,15},{152,16... | collective-permute-start | bytes 4718600 | tf_op jit(solution)/shard_map/ppermute | solution.py:53
  146.8 36.4 %collective-permute-start.21 = (bf16[2,4,384,256]{3,2,1,0:T(8,128)(2,1)}, bf16[2,4,384,256]{3,2,1,0:T(8,128)(2,1)S(1)}, u32[]{:S(2)}, u32[]{:S(2)}) collective-permute-start(bf16[2,4,384,256]{3,2,1,0:T(8,128)(2,1)} %get-tuple-element.65), channel_id=1, source_target_pairs={{8,0},{10,2},{12,4},{14,6},{129,9},{131,11},{133,13},{135,15},{24,... | collective-permute-start | bytes 4718600 | tf_op jit(solution)/shard_map/ppermute | solution.py:53
  148.8 20.0 %collective-permute-start.15 = (bf16[4,384,256]{2,1,0:T(8,128)(2,1)S(1)}, bf16[4,384,256]{2,1,0:T(8,128)(2,1)S(1)}, u32[]{:S(2)}, u32[]{:S(2)}) collective-permute-start(bf16[4,384,256]{2,1,0:T(8,128)(2,1)S(1)} %add_convert_fusion.2), channel_id=1, source_target_pairs={{0,6},{1,7},{2,0},{3,1},{4,2},{5,3},{6,4},{7,5},{8,14},{9,15},{10,... | collective-permute-start | bytes 2359304 | tf_op jit(solution)/shard_map/ppermute | solution.py:53
  151.7 20.9 %collective-permute-start.13 = (bf16[4,384,256]{2,1,0:T(8,128)(2,1)S(1)}, bf16[4,384,256]{2,1,0:T(8,128)(2,1)S(1)}, u32[]{:S(2)}, u32[]{:S(2)}) collective-permute-start(bf16[4,384,256]{2,1,0:T(8,128)(2,1)S(1)} %add_convert_fusion.3), channel_id=1, source_target_pairs={{0,2},{1,3},{2,4},{3,5},{4,6},{5,7},{6,0},{7,1},{8,10},{9,11},{10,... | collective-permute-start | bytes 2359304 | tf_op jit(solution)/shard_map/ppermute | solution.py:53
  173.0 16.9 %collective-permute-start.18 = (bf16[2,384,256]{2,1,0:T(8,128)(2,1)S(1)}, bf16[2,384,256]{2,1,0:T(8,128)(2,1)}, u32[]{:S(2)}, u32[]{:S(2)}) collective-permute-start(bf16[2,384,256]{2,1,0:T(8,128)(2,1)S(1)} %get-tuple-element.77), channel_id=1, source_target_pairs={{0,128},{2,130},{4,132},{6,134},{9,137},{11,139},{13,141},{15,143}... | collective-permute-start | bytes 1179656 | tf_op jit(solution)/shard_map/ppermute | solution.py:53
  174.6 15.3 %collective-permute-start.17 = (bf16[2,384,256]{2,1,0:T(8,128)(2,1)S(1)}, bf16[2,384,256]{2,1,0:T(8,128)(2,1)}, u32[]{:S(2)}, u32[]{:S(2)}) collective-permute-start(bf16[2,384,256]{2,1,0:T(8,128)(2,1)S(1)} %get-tuple-element.77), channel_id=1, source_target_pairs={{136,0},{138,2},{140,4},{142,6},{1,9},{3,11},{5,13},{7,15},{152,16... | collective-permute-start | bytes 1179656 | tf_op jit(solution)/shard_map/ppermute | solution.py:53
  176.6 13.3 %collective-permute-start.16 = (bf16[2,384,256]{2,1,0:T(8,128)(2,1)S(1)}, bf16[2,384,256]{2,1,0:T(8,128)(2,1)}, u32[]{:S(2)}, u32[]{:S(2)}) collective-permute-start(bf16[2,384,256]{2,1,0:T(8,128)(2,1)S(1)} %get-tuple-element.76), channel_id=1, source_target_pairs={{8,0},{10,2},{12,4},{14,6},{129,9},{131,11},{133,13},{135,15},{24,... | collective-permute-start | bytes 1179656 | tf_op jit(solution)/shard_map/ppermute | solution.py:53
  191.4 9.5 %collective-permute-start.19 = (bf16[384,256]{1,0:T(8,128)(2,1)S(1)}, bf16[384,256]{1,0:T(8,128)(2,1)S(1)}, u32[]{:S(2)}, u32[]{:S(2)}) collective-permute-start(bf16[384,256]{1,0:T(8,128)(2,1)S(1)} %slice_bitcast_fusion.5), channel_id=1, source_target_pairs={{0,1},{2,3},{4,5},{6,7},{9,8},{11,10},{13,12},{15,14},{16,17},{18,... | collective-permute-start | bytes 589832 | tf_op jit(solution)/shard_map/ppermute | solution.py:53
  192.7 10.9 %collective-permute-start.28 = (bf16[1152,256]{1,0:T(8,128)(2,1)S(1)}, bf16[1152,256]{1,0:T(8,128)(2,1)S(1)}, u32[]{:S(2)}, u32[]{:S(2)}) collective-permute-start(bf16[1152,256]{1,0:T(8,128)(2,1)S(1)} %copy-done.14), channel_id=1, source_target_pairs={{8,0},{136,1},{10,2},{138,3},{12,4},{140,5},{14,6},{142,7},{128,8}... | collective-permute-start | bytes 1769480 | tf_op jit(solution)/shard_map/ppermute | solution.py:53
  196.6 10.0 %collective-permute-start.27 = (bf16[384,256]{1,0:T(8,128)(2,1)S(1)}, bf16[384,256]{1,0:T(8,128)(2,1)S(1)}, u32[]{:S(2)}, u32[]{:S(2)}) collective-permute-start(bf16[384,256]{1,0:T(8,128)(2,1)S(1)} %get-tuple-element.74), channel_id=1, source_target_pairs={{0,4},{1,5},{2,6},{3,7},{4,0},{5,1},{6,2},{7,3},{8,12},{9,13},{10,... | collective-permute-start | bytes 589832 | tf_op jit(solution)/shard_map/ppermute | solution.py:53
  199.4 9.6 %collective-permute-start.26 = (bf16[384,256]{1,0:T(8,128)(2,1)S(1)}, bf16[384,256]{1,0:T(8,128)(2,1)S(1)}, u32[]{:S(2)}, u32[]{:S(2)}) collective-permute-start(bf16[384,256]{1,0:T(8,128)(2,1)S(1)} %get-tuple-element.75), channel_id=1, source_target_pairs={{0,6},{1,7},{2,0},{3,1},{4,2},{5,3},{6,4},{7,5},{8,14},{9,15},{10,... | collective-permute-start | bytes 589832 | tf_op jit(solution)/shard_map/ppermute | solution.py:53
  (24 other events, 198.4 us)
Sparse Core Ops, SparseCore 0:
  21.2 62.9 all-gather.2
  129.8 58.5 reduce-scatter.1

commit v2 on v1

--- a/solution.py
+++ b/solution.py
@@ -11,7 +11,7 @@
 ZN, YN = 8, 4
 BF = jnp.bfloat16
 F32 = jnp.float32
-VMEM_BYTES = 60 * 1024 * 1024
+VMEM_BYTES = 63 * 1024 * 1024
 
 
 def position(device):
@@ -91,7 +91,7 @@
     return lax.dot_general(a, b, (((da,), (db,)), ((), ())), preferred_element_type=F32)
 
 
-def call(kernel, outs, scratch, n_sems, args, name, out_space=VMEM, near=()):
+def call(kernel, outs, scratch, n_sems, args, name, out_space=VMEM, near=(), traffic=1000):
     return pl.pallas_call(
         kernel,
         out_shape=outs,
@@ -99,7 +99,7 @@
         out_specs=jax.tree.map(lambda _: out_space, outs),
         scratch_shapes=[*scratch, pltpu.SemaphoreType.DMA((n_sems,))],
         compiler_params=pltpu.CompilerParams(vmem_limit_bytes=VMEM_BYTES),
-        cost_estimate=pl.CostEstimate(flops=1000, bytes_accessed=1000, transcendentals=0),
+        cost_estimate=pl.CostEstimate(flops=1000, bytes_accessed=traffic, transcendentals=0),
         name=name,
     )(*args)
 
@@ -170,40 +170,27 @@
     return call(hidden_cot_kernel, outs, scratch, 10, (idx, local, remote, w), "hidden_cots")
 
 
-def activation_kernel(own, far, hidden, activated, slope):
+def activation_kernel(own, far, hc_own, hc_far, hidden, cots):
     gate = own[:, :384] + far[:, :384]
     linear = own[:, 384:] + far[:, 384:]
     k = 0.7978845608028654
     t = jnp.tanh(k * (gate + 0.044715 * gate * gate * gate))
     half = 0.5 * (1.0 + t)
-    value = gate * half
-    activated[...] = value
-    hidden[...] = (value * linear).astype(BF)
-    slope[...] = linear * (half + 0.5 * gate * (1.0 - t * t) * (k * (1.0 + 3 * 0.044715 * gate * gate)))
-
-
-def activation(own, far):
+    activated = gate * half
+    slope = half + 0.5 * gate * (1.0 - t * t) * (k * (1.0 + 3 * 0.044715 * gate * gate))
+    hidden[...] = (activated * linear).astype(BF)
+    cot = hc_own[...] + hc_far[...]
+    cots[:, :384] = (cot * linear * slope).astype(BF)
+    cots[:, 384:] = (cot * activated).astype(BF)
+
+
+def activation(own, far, hc_own, hc_far):
     return pl.pallas_call(
         activation_kernel,
-        out_shape=[shape(384, 384), shape(384, 384, dtype=F32), shape(384, 384, dtype=F32)],
+        out_shape=[shape(384, 384), shape(384, 768)],
         cost_estimate=pl.CostEstimate(flops=1000, bytes_accessed=1000, transcendentals=0),
         name="activation",
-    )(own, far)
-
-
-def cot_kernel(own, far, activated, slope, cots):
-    cot = own[...] + far[...]
-    cots[:, :384] = (cot * slope[...]).astype(BF)
-    cots[:, 384:] = (cot * activated[...]).astype(BF)
-
-
-def cotangents(own, far, activated, slope):
-    return pl.pallas_call(
-        cot_kernel,
-        out_shape=shape(384, 768),
-        cost_estimate=pl.CostEstimate(flops=1000, bytes_accessed=1000, transcendentals=0),
-        name="cotangents",
-    )(own, far, activated, slope)
+    )(own, far, hc_own, hc_far)
 
 
 def stack_tokens(idx, own, other, dst):
@@ -220,22 +207,19 @@
     pieces = refs[:4]
     out, ht, ct, ds, xs, stage, sems = refs[4:]
     copies = Copies(sems)
-    out_cots = cot_copies(copies, idx, local, remote, ds)
-    arriving = []
+    loads = cot_copies(copies, idx, local, remote, ds)
     for piece, step in zip(pieces, STEPS):
-        for core in range(2):
-            j = column(idx, step, core)
-            both = [copies.start(piece.at[slot], xs.at[rows_of(token_of(idx, slot)), block(j)]) for slot in (core, 2 + core)]
-            arriving.append((j, both))
+        for slot in range(4):
+            dst = xs.at[rows_of(token_of(idx, slot)), block(column(idx, step, slot))]
+            loads.append(copies.start(piece.at[slot], dst))
     transposed(idx, hidden, hidden_far, ht)
     transposed(idx, cots, cots_far, ct)
-    wait(out_cots)
+    wait(loads)
+    leaving = []
     for j in range(ZN):
-        stage[j, 768:] = dot(ht[...], ds[:, 256 * j : 256 * j + 256]).astype(BF)
-    leaving = []
-    for j, both in arriving:
-        wait(both)
-        stage[j, :768] = dot(ct[...], xs[:, block(j)]).astype(BF)
+        columns = slice(256 * j, 256 * j + 256)
+        stage[j, :768] = dot(ct[...], xs[:, columns]).astype(BF)
+        stage[j, 768:] = dot(ht[...], ds[:, columns]).astype(BF)
         leaving.append(copies.start(stage.at[j], out.at[j]))
     wait(leaving)
 
@@ -264,7 +248,7 @@
 def outputs(idx, own, other, w):
     outs = [shape(4, 384, 256)] * 3 + [shape(2, 384, 256)] * 2
     scratch = [pltpu.VMEM((768, 384), BF), pltpu.VMEM((384, 2048), BF)]
-    return call(output_kernel, outs, scratch, 8, (idx, own, other, w), "outputs", near=(1, 2))
+    return call(output_kernel, outs, scratch, 8, (idx, own, other, w), "outputs", near=(1, 2), traffic=40_000_000)
 
 
 def input_grad_kernel(idx, own, other, w, first, second, cs, ws, sf, ss, sems):
@@ -346,19 +330,16 @@
     far = move(far, CORE)
     hc_far, hc_own = hidden_cots(idx, out_cotangent, remote, w)
     hc_far = move(hc_far, CORE)
-    hidden, activated, slope = activation(own, far)
+    hidden, cots = activation(own, far, hc_own, hc_far)
     hidden_far = move(hidden, CORE)
-    hc_far, activated = lax.optimization_barrier((hc_far, activated))
-    cots = cotangents(hc_own, hc_far, activated, slope)
     cots_far = move(cots, CORE)
 
-    hidden_far, cots = lax.optimization_barrier((hidden_far, cots))
-    here, up, down, across_up, across_down = outputs(idx, hidden, hidden_far, w)
-    idx, across_up, across_down = lax.optimization_barrier((idx, across_up, across_down))
     parts = weight_grads(idx, hidden, hidden_far, cots, cots_far, out_cotangent, remote, x)
     idx, parts = lax.optimization_barrier((idx, parts))
     share = lax.psum_scatter(parts.reshape(8 * 1152, 256), "dp", scatter_dimension=0, axis_index_groups=Z_GROUPS, tiled=True)
     first, second = input_grads(idx, cots, cots_far, w)
+    idx, first, second = lax.optimization_barrier((idx, first, second))
+    here, up, down, across_up, across_down = outputs(idx, hidden, hidden_far, w)
 
     zero = jnp.zeros((), BF)
     up = add(up, lax.pad(move(across_up, Y_STEPS[0]), zero, ((0, 2, 0), (0, 0, 0), (0, 0, 0))))

time: 217 us -> 212 us (0.977)
  starting transfers between devices: 45.9 us -> 60.8 us
  waiting for transfers between devices: 91.8 us -> 79 us
  Pallas kernels: 48.2 us -> 43.2 us
  local copies, waits for them, and re-layouts: 10.8 us -> 7.73 us
    ppermute x29, starting transfers between devices: 45.9 us -> 60.7 us  [move(): return lax.ppermute(value, AXES, pairs)]
    ppermute x29, waiting for transfers between devices: 77.7 us -> 71.1 us  [move(): return lax.ppermute(value, AXES, pairs)]
    reduce_scatter x1, waiting for transfers between devices: 4.36 us -> 0.02 us  [per_device(): lax.psum_scatter(parts.reshape(8 * 1152, 256), 'dp', scatter_dimension=0,...]
    unnamed x34 -> x26, local copies, waits for them, and re-layouts: 7.22 us -> 4.09 us
    pallas_call x5, Pallas kernels: 38.5 us -> 35.6 us  [call(): pl.pallas_call(kernel, out_shape=outs, in_specs=[SMEM] + [VMEM if i in ne...]
    pallas_call x1 -> x0, Pallas kernels: 2.55 us -> none  [cotangents(): pl.pallas_call(cot_kernel, out_shape=shape(384, 768), cost_estimate=pl.Co...]
  transfers between devices with their start and end apart: 31 -> 31, of which waited for: 15 -> 15; matrix products, arithmetic and copies ran while one was open for 4% -> 5% of each run, Pallas kernels for 14% -> 13%
where the time goes in v2:
time: 212 us
  waiting for transfers between devices  79 us (37%)
  starting transfers between devices  60.8 us (29%)
  Pallas kernels  43.2 us (20%)
  between operations  14.4 us (7%)
  local copies, waits for them, and re-layouts  7.73 us (4%)
  other arithmetic  6.67 us (3%)
    ppermute x29, waiting for transfers between devices, move(): return lax.ppermute(value, AXES, pairs)  71.1 us
    ppermute x29, starting transfers between devices, move(): return lax.ppermute(value, AXES, pairs)  60.7 us
    pallas_call x5, Pallas kernels, call(): pl.pallas_call(kernel, out_shape=outs, in_specs=[SMEM] + [VMEM if i in ne...  35.6 us
    all_gather x1, waiting for transfers between devices, per_device(): w = lax.all_gather(shard, 'dp', axis_index_groups=Z_GROUPS)  7.76 us
    convert_element_type x6, other arithmetic, add(): return functools.reduce(jnp.add, [t.astype(F32) for t in terms]).astype(BF)  4.77 us
  transfers between devices with their start and end apart: 31, of which 15 were waited for; matrix products, arithmetic and copies ran while one was open for 5% of the time, Pallas kernels for 13%

profile of v2, /device:TPU:1, one launch (start us, length us, event | category | flops | bytes accessed | tf_op | source)
XLA Modules:
  0.0 211.7 jit_solution(4885671018830455063)
XLA Ops:
  9.2 3.9 %collective-permute-start = (bf16[1152,256]{1,0:T(8,128)(2,1)}, bf16[1152,256]{1,0:T(8,128)(2,1)S(1)}, u32[]{:S(2)}, u32[]{:S(2)}) collective-permute-start(bf16[1152,256]{1,0:T(8,128)(2,1)} %pack.1), channel_id=1, source_target_pairs={{0,8},{1,136},{2,10},{3,138},{4,12},{5,140},{6,14},{7,142},{8,128}... | collective-permute-start | bytes 1769480 | tf_op jit(solution)/shard_map/ppermute | solution.py:53
  16.6 3.6 %collective-permute-done = bf16[1152,256]{1,0:T(8,128)(2,1)S(1)} collective-permute-done((bf16[1152,256]{1,0:T(8,128)(2,1)}, bf16[1152,256]{1,0:T(8,128)(2,1)S(1)}, u32[]{:S(2)}, u32[]{:S(2)}) %collective-permute-start) | collective-permute-done | bytes 589856 | tf_op jit(solution)/shard_map/ppermute | solution.py:53
  24.4 2.8 %constant_dynamic-slice_fusion = bf16[384,2048]{1,0:T(8,128)(2,1)} fusion(bf16[384,4096]{1,0:T(8,128)(2,1)} %local.3, s32[]{:T(128)S(6)} %select_n.70), kind=kLoop, calls=%fused_computation.22 | loop fusion | bytes 3145732 | tf_op jit(solution)/shard_map/dynamic_slice | solution.py:322
  27.3 3.6 %collective-permute-done.2 = bf16[2,384,256]{2,1,0:T(8,128)(2,1)S(1)} collective-permute-done((bf16[2,384,256]{2,1,0:T(8,128)(2,1)S(1)}, bf16[2,384,256]{2,1,0:T(8,128)(2,1)S(1)}, u32[]{:S(2)}, u32[]{:S(2)}) %collective-permute-start.2) | collective-permute-done | bytes 393248 | tf_op jit(solution)/shard_map/ppermute | solution.py:53
  31.7 6.8 %collective-permute-start.9 = (bf16[384,2048]{1,0:T(8,128)(2,1)}, bf16[384,2048]{1,0:T(8,128)(2,1)}, u32[]{:S(2)}, u32[]{:S(2)}) collective-permute-start(bf16[384,2048]{1,0:T(8,128)(2,1)} %constant_dynamic-slice_fusion), channel_id=1, source_target_pairs={{0,136},{1,137},{2,138},{3,139},{4,140},{5,141},{6,142},{7,143},{8... | collective-permute-start | bytes 4718600 | tf_op jit(solution)/shard_map/ppermute | solution.py:53
  38.5 2.9 %collective-permute-start.7 = (bf16[4,384,256]{2,1,0:T(8,128)(2,1)S(1)}, bf16[4,384,256]{2,1,0:T(8,128)(2,1)S(1)}, u32[]{:S(2)}, u32[]{:S(2)}) collective-permute-start(bf16[4,384,256]{2,1,0:T(8,128)(2,1)S(1)} %pad_maximum_fusion.refs_0_), channel_id=1, source_target_pairs={{0,4},{1,5},{2,6},{3,7},{4,0},{5,1},{6,2},{7,3},{8,12},{9,13},{10,... | collective-permute-start | bytes 2359304 | tf_op jit(solution)/shard_map/ppermute | solution.py:53
  43.5 12.3 %collective-permute-done.7.refs_3_ = bf16[4,384,256]{2,1,0:T(8,128)(2,1)S(1)} collective-permute-done((bf16[4,384,256]{2,1,0:T(8,128)(2,1)S(1)}, bf16[4,384,256]{2,1,0:T(8,128)(2,1)S(1)}, u32[]{:S(2)}, u32[]{:S(2)}) %collective-permute-start.7) | collective-permute-done | bytes 786464 | tf_op jit(solution)/shard_map/ppermute | solution.py:53
  55.9 19.8 %collective-permute-done.6.refs_2_ = bf16[4,384,256]{2,1,0:T(8,128)(2,1)S(1)} collective-permute-done((bf16[4,384,256]{2,1,0:T(8,128)(2,1)S(1)}, bf16[4,384,256]{2,1,0:T(8,128)(2,1)S(1)}, u32[]{:S(2)}, u32[]{:S(2)}) %collective-permute-start.6) | collective-permute-done | bytes 786464 | tf_op jit(solution)/shard_map/ppermute | solution.py:53
  76.4 7.8 %all-gather.3.cloned.1.call-done = bf16[9216,256]{1,0:T(8,128)(2,1)} async-done(((bf16[1152,256]{1,0:T(8,128)(2,1)}), bf16[9216,256]{1,0:T(8,128)(2,1)}) %all-gather.3.cloned.1.call-update) | async-done | bytes 4718608 | tf_op jit(solution)/shard_map/all_gather | solution.py:320
  84.2 8.4 %projections.1 = (f32[384,768]{1,0:T(8,128)}, f32[384,768]{1,0:T(8,128)}) custom-call(s32[6]{0:T(128)} %stack.36.idx, bf16[4,384,256]{2,1,0:T(8,128)(2,1)} %copy-done, bf16[4,384,256]{2,1,0:T(8,128)(2,1)} %copy-done.3, bf16[4,384,256]{2,1,0:T(8,128)(2,1)} %copy-done.2, bf16[4,384,256]{2,1,0:T(8,128)(2,1)} %copy-done.1, bf16[8,1152,256]{2,1,0:T(8,128)(2,1)} %bitcast.31), custom_call_target="tpu_custom_call" | custom-call | flops 1000 | bytes 1000 | tf_op jit(solution)/shard_map/projections/pallas_call | solution.py:95
  93.3 5.7 %hidden_cots.1 = (f32[384,384]{1,0:T(8,128)}, f32[384,384]{1,0:T(8,128)}) custom-call(s32[6]{0:T(128)} %stack.36.idx, bf16[384,4096]{1,0:T(8,128)(2,1)} %local.3, bf16[384,2048]{1,0:T(8,128)(2,1)} %collective-permute-done.9.remote, bf16[8,1152,256]{2,1,0:T(8,128)(2,1)} %bitcast.32), custom_call_target="tpu_custom_call" | custom-call | flops 1000 | bytes 1000 | tf_op jit(solution)/shard_map/hidden_cots/pallas_call | solution.py:95
  102.2 3.3 %activation.1 = (bf16[384,384]{1,0:T(8,128)(2,1)}, bf16[384,768]{1,0:T(8,128)(2,1)}) custom-call(f32[384,768]{1,0:T(8,128)} %get-tuple-element.39.own, f32[384,768]{1,0:T(8,128)} %collective-permute-done.8.far, f32[384,384]{1,0:T(8,128)} %get-tuple-element.42.hc_own, f32[384,384]{1,0:T(8,128)} %copy-done.9), custom_call_target="tpu_custom_call" | custom-call | flops 1000 | bytes 1000 | tf_op jit(solution)/shard_map/activation/pallas_call | solution.py:188
  109.7 9.4 %weight_grads.1 = bf16[8,1152,256]{2,1,0:T(8,128)(2,1)} custom-call(s32[6]{0:T(128)} %stack.36.idx, bf16[384,384]{1,0:T(8,128)(2,1)} %get-tuple-element.44.hidden.own, bf16[384,384]{1,0:T(8,128)(2,1)} %copy-done.6, bf16[384,768]{1,0:T(8,128)(2,1)} %get-tuple-element.45.cots.own, bf16[384,768]{1,0:T(8,128)(2,1)} %copy-done.4, bf16[384,4096]{1,0:T(8,128)(2,1)} %local.3, ...), custom_call_target="tpu_custom_call" | custom-call | flops 1000 | bytes 1000 | tf_op jit(solution)/shard_map/weight_grads/pallas_call | solution.py:95
  119.2 6.7 %input_grads.1 = (bf16[2,4,384,256]{3,2,1,0:T(8,128)(2,1)}, bf16[2,4,384,256]{3,2,1,0:T(8,128)(2,1)}) custom-call(s32[6]{0:T(128)} %stack.36.idx, bf16[384,768]{1,0:T(8,128)(2,1)} %get-tuple-element.45.cots.own, bf16[384,768]{1,0:T(8,128)(2,1)} %copy-done.4, bf16[8,1152,256]{2,1,0:T(8,128)(2,1)} %bitcast.33), custom_call_target="tpu_custom_call" | custom-call | flops 1000 | bytes 1000 | tf_op jit(solution)/shard_map/input_grads/pallas_call | solution.py:95
  125.9 5.5 %outputs.1 = (bf16[4,384,256]{2,1,0:T(8,128)(2,1)}, bf16[4,384,256]{2,1,0:T(8,128)(2,1)}, bf16[4,384,256]{2,1,0:T(8,128)(2,1)}, bf16[2,384,256]{2,1,0:T(8,128)(2,1)}, bf16[2,384,256]{2,1,0:T(8,128)(2,1)}) custom-call(s32[6]{0:T(128)} %stack.36.idx, bf16[384,384]{1,0:T(8,128)(2,1)} %get-tuple-element.44.hidden.own, bf16[384,384]{1,0:T(8,128)(2,1)} %copy-done.6, ...), custom_call_target="tpu_custom_call" | custom-call | flops 1000 | bytes 40000000 | tf_op jit(solution)/shard_map/outputs/pallas_call | solution.py:95
  134.7 6.1 %collective-permute-start.22 = (bf16[2,4,384,256]{3,2,1,0:T(8,128)(2,1)}, bf16[2,4,384,256]{3,2,1,0:T(8,128)(2,1)S(1)}, u32[]{:S(2)}, u32[]{:S(2)}) collective-permute-start(bf16[2,4,384,256]{3,2,1,0:T(8,128)(2,1)} %get-tuple-element.56), channel_id=1, source_target_pairs={{136,0},{138,2},{140,4},{142,6},{1,9},{3,11},{5,13},{7,15},{152,16... | collective-permute-start | bytes 4718600 | tf_op jit(solution)/shard_map/ppermute | solution.py:53
  144.1 3.3 %collective-permute-start.16 = (bf16[4,384,256]{2,1,0:T(8,128)(2,1)S(1)}, bf16[4,384,256]{2,1,0:T(8,128)(2,1)S(1)}, u32[]{:S(2)}, u32[]{:S(2)}) collective-permute-start(bf16[4,384,256]{2,1,0:T(8,128)(2,1)S(1)} %add_convert_fusion.2), channel_id=1, source_target_pairs={{0,6},{1,7},{2,0},{3,1},{4,2},{5,3},{6,4},{7,5},{8,14},{9,15},{10,... | collective-permute-start | bytes 2359304 | tf_op jit(solution)/shard_map/ppermute | solution.py:53
  147.6 15.8 %collective-permute-done.16 = bf16[4,384,256]{2,1,0:T(8,128)(2,1)S(1)} collective-permute-done((bf16[4,384,256]{2,1,0:T(8,128)(2,1)S(1)}, bf16[4,384,256]{2,1,0:T(8,128)(2,1)S(1)}, u32[]{:S(2)}, u32[]{:S(2)}) %collective-permute-start.16) | collective-permute-done | bytes 786464 | tf_op jit(solution)/shard_map/ppermute | solution.py:53
  163.4 3.4 %collective-permute-done.14 = bf16[4,384,256]{2,1,0:T(8,128)(2,1)S(1)} collective-permute-done((bf16[4,384,256]{2,1,0:T(8,128)(2,1)S(1)}, bf16[4,384,256]{2,1,0:T(8,128)(2,1)S(1)}, u32[]{:S(2)}, u32[]{:S(2)}) %collective-permute-start.14) | collective-permute-done | bytes 786464 | tf_op jit(solution)/shard_map/ppermute | solution.py:53
  168.8 6.2 %collective-permute-start.18 = (bf16[2,384,256]{2,1,0:T(8,128)(2,1)S(1)}, bf16[2,384,256]{2,1,0:T(8,128)(2,1)}, u32[]{:S(2)}, u32[]{:S(2)}) collective-permute-start(bf16[2,384,256]{2,1,0:T(8,128)(2,1)S(1)} %get-tuple-element.67), channel_id=1, source_target_pairs={{136,0},{138,2},{140,4},{142,6},{1,9},{3,11},{5,13},{7,15},{152,16... | collective-permute-start | bytes 1179656 | tf_op jit(solution)/shard_map/ppermute | solution.py:53
  175.0 4.5 %collective-permute-start.17 = (bf16[2,384,256]{2,1,0:T(8,128)(2,1)S(1)}, bf16[2,384,256]{2,1,0:T(8,128)(2,1)}, u32[]{:S(2)}, u32[]{:S(2)}) collective-permute-start(bf16[2,384,256]{2,1,0:T(8,128)(2,1)S(1)} %get-tuple-element.66), channel_id=1, source_target_pairs={{8,0},{10,2},{12,4},{14,6},{129,9},{131,11},{133,13},{135,15},{24,... | collective-permute-start | bytes 1179656 | tf_op jit(solution)/shard_map/ppermute | solution.py:53
  186.2 3.7 %collective-permute-start.28 = (bf16[1152,256]{1,0:T(8,128)(2,1)S(1)}, bf16[1152,256]{1,0:T(8,128)(2,1)S(1)}, u32[]{:S(2)}, u32[]{:S(2)}) collective-permute-start(bf16[1152,256]{1,0:T(8,128)(2,1)S(1)} %copy-done.12), channel_id=1, source_target_pairs={{8,0},{136,1},{10,2},{138,3},{12,4},{140,5},{14,6},{142,7},{128,8}... | collective-permute-start | bytes 1769480 | tf_op jit(solution)/shard_map/ppermute | solution.py:53
  191.1 4.8 %collective-permute-start.27 = (bf16[384,256]{1,0:T(8,128)(2,1)S(1)}, bf16[384,256]{1,0:T(8,128)(2,1)S(1)}, u32[]{:S(2)}, u32[]{:S(2)}) collective-permute-start(bf16[384,256]{1,0:T(8,128)(2,1)S(1)} %get-tuple-element.64), channel_id=1, source_target_pairs={{0,4},{1,5},{2,6},{3,7},{4,0},{5,1},{6,2},{7,3},{8,12},{9,13},{10,... | collective-permute-start | bytes 589832 | tf_op jit(solution)/shard_map/ppermute | solution.py:53
  200.2 3.9 %collective-permute-done.27 = bf16[384,256]{1,0:T(8,128)(2,1)S(1)} collective-permute-done((bf16[384,256]{1,0:T(8,128)(2,1)S(1)}, bf16[384,256]{1,0:T(8,128)(2,1)S(1)}, u32[]{:S(2)}, u32[]{:S(2)}) %collective-permute-start.27) | collective-permute-done | bytes 196640 | tf_op jit(solution)/shard_map/ppermute | solution.py:53
  (92 shorter events, 43.0 us)
Async XLA Ops:
  7.2 77.0 %all-gather.3.cloned.1.call-start = ((), (), s32[]{:S(2)}) async-start(), calls=%async_computation.2 | async-start | bytes 5308416 | tf_op jit(solution)/shard_map/all_gather | solution.py:320
  9.2 11.0 %collective-permute-start = (bf16[1152,256]{1,0:T(8,128)(2,1)}, bf16[1152,256]{1,0:T(8,128)(2,1)S(1)}, u32[]{:S(2)}, u32[]{:S(2)}) collective-permute-start(bf16[1152,256]{1,0:T(8,128)(2,1)} %pack.1), channel_id=1, source_target_pairs={{0,8},{1,136},{2,10},{3,138},{4,12},{5,140},{6,14},{7,142},{8,128}... | collective-permute-start | bytes 1769480 | tf_op jit(solution)/shard_map/ppermute | solution.py:53
  21.1 159.3 %reduce-scatter.2.cloned.1.call-start = ((), (), s32[]{:S(2)}) async-start(), calls=%async_computation.1 | async-start | bytes 5308416 | tf_op jit(solution)/shard_map/reduce_scatter | solution.py:339
  21.1 9.7 %collective-permute-start.2 = (bf16[2,384,256]{2,1,0:T(8,128)(2,1)S(1)}, bf16[2,384,256]{2,1,0:T(8,128)(2,1)S(1)}, u32[]{:S(2)}, u32[]{:S(2)}) collective-permute-start(bf16[2,384,256]{2,1,0:T(8,128)(2,1)S(1)} %pad_maximum_fusion.1), channel_id=1, source_target_pairs={{0,8},{2,10},{4,12},{6,14},{9,129},{11,131},{13,133},{15,135},{16,... | collective-permute-start | bytes 1179656 | tf_op jit(solution)/shard_map/ppermute | solution.py:53
  22.4 9.1 %collective-permute-start.4 = (bf16[2,384,256]{2,1,0:T(8,128)(2,1)S(1)}, bf16[2,384,256]{2,1,0:T(8,128)(2,1)S(1)}, u32[]{:S(2)}, u32[]{:S(2)}) collective-permute-start(bf16[2,384,256]{2,1,0:T(8,128)(2,1)S(1)} %pad_maximum_fusion.1), channel_id=1, source_target_pairs={{0,136},{2,138},{4,140},{6,142},{9,1},{11,3},{13,5},{15,7},{16,152... | collective-permute-start | bytes 1179656 | tf_op jit(solution)/shard_map/ppermute | solution.py:53
  31.7 61.6 %collective-permute-start.9 = (bf16[384,2048]{1,0:T(8,128)(2,1)}, bf16[384,2048]{1,0:T(8,128)(2,1)}, u32[]{:S(2)}, u32[]{:S(2)}) collective-permute-start(bf16[384,2048]{1,0:T(8,128)(2,1)} %constant_dynamic-slice_fusion), channel_id=1, source_target_pairs={{0,136},{1,137},{2,138},{3,139},{4,140},{5,141},{6,142},{7,143},{8... | collective-permute-start | bytes 4718600 | tf_op jit(solution)/shard_map/ppermute | solution.py:53
  38.5 17.3 %collective-permute-start.7 = (bf16[4,384,256]{2,1,0:T(8,128)(2,1)S(1)}, bf16[4,384,256]{2,1,0:T(8,128)(2,1)S(1)}, u32[]{:S(2)}, u32[]{:S(2)}) collective-permute-start(bf16[4,384,256]{2,1,0:T(8,128)(2,1)S(1)} %pad_maximum_fusion.refs_0_), channel_id=1, source_target_pairs={{0,4},{1,5},{2,6},{3,7},{4,0},{5,1},{6,2},{7,3},{8,12},{9,13},{10,... | collective-permute-start | bytes 2359304 | tf_op jit(solution)/shard_map/ppermute | solution.py:53
  41.4 34.2 %collective-permute-start.6 = (bf16[4,384,256]{2,1,0:T(8,128)(2,1)S(1)}, bf16[4,384,256]{2,1,0:T(8,128)(2,1)S(1)}, u32[]{:S(2)}, u32[]{:S(2)}) collective-permute-start(bf16[4,384,256]{2,1,0:T(8,128)(2,1)S(1)} %pad_maximum_fusion.refs_0_), channel_id=1, source_target_pairs={{0,6},{1,7},{2,0},{3,1},{4,2},{5,3},{6,4},{7,5},{8,14},{9,15},{10,... | collective-permute-start | bytes 2359304 | tf_op jit(solution)/shard_map/ppermute | solution.py:53
  42.2 34.2 %collective-permute-start.5 = (bf16[4,384,256]{2,1,0:T(8,128)(2,1)S(1)}, bf16[4,384,256]{2,1,0:T(8,128)(2,1)S(1)}, u32[]{:S(2)}, u32[]{:S(2)}) collective-permute-start(bf16[4,384,256]{2,1,0:T(8,128)(2,1)S(1)} %pad_maximum_fusion.refs_0_), channel_id=1, source_target_pairs={{0,2},{1,3},{2,4},{3,5},{4,6},{5,7},{6,0},{7,1},{8,10},{9,11},{10,... | collective-permute-start | bytes 2359304 | tf_op jit(solution)/shard_map/ppermute | solution.py:53
  92.6 8.7 %collective-permute-start.8 = (f32[384,768]{1,0:T(8,128)}, f32[384,768]{1,0:T(8,128)}, u32[]{:S(2)}, u32[]{:S(2)}) collective-permute-start(f32[384,768]{1,0:T(8,128)} %get-tuple-element.40), channel_id=1, source_target_pairs={{0,1},{1,0},{2,3},{3,2},{4,5},{5,4},{6,7},{7,6},{8,9},{9,8},{10,11... | collective-permute-start | bytes 3538952 | tf_op jit(solution)/shard_map/ppermute | solution.py:53
  131.4 11.3 %collective-permute-start.15 = (bf16[2,384,256]{2,1,0:T(8,128)(2,1)}, bf16[2,384,256]{2,1,0:T(8,128)(2,1)S(1)}, u32[]{:S(2)}, u32[]{:S(2)}) collective-permute-start(bf16[2,384,256]{2,1,0:T(8,128)(2,1)} %get-tuple-element.54), channel_id=1, source_target_pairs={{0,6},{1,7},{2,0},{3,1},{4,2},{5,3},{6,4},{7,5},{8,14},{9,15},{10,... | collective-permute-start | bytes 1179656 | tf_op jit(solution)/shard_map/ppermute | solution.py:53
  133.9 13.5 %collective-permute-start.13 = (bf16[2,384,256]{2,1,0:T(8,128)(2,1)}, bf16[2,384,256]{2,1,0:T(8,128)(2,1)S(1)}, u32[]{:S(2)}, u32[]{:S(2)}) collective-permute-start(bf16[2,384,256]{2,1,0:T(8,128)(2,1)} %get-tuple-element.52), channel_id=1, source_target_pairs={{0,2},{1,3},{2,4},{3,5},{4,6},{5,7},{6,0},{7,1},{8,10},{9,11},{10,... | collective-permute-start | bytes 1179656 | tf_op jit(solution)/shard_map/ppermute | solution.py:53
  133.9 45.6 %collective-permute-start.23 = (bf16[2,4,384,256]{3,2,1,0:T(8,128)(2,1)}, bf16[2,4,384,256]{3,2,1,0:T(8,128)(2,1)S(1)}, u32[]{:S(2)}, u32[]{:S(2)}) collective-permute-start(bf16[2,4,384,256]{3,2,1,0:T(8,128)(2,1)} %get-tuple-element.56), channel_id=1, source_target_pairs={{0,128},{2,130},{4,132},{6,134},{9,137},{11,139},{13,141},{15,143}... | collective-permute-start | bytes 4718600 | tf_op jit(solution)/shard_map/ppermute | solution.py:53
  134.7 44.8 %collective-permute-start.22 = (bf16[2,4,384,256]{3,2,1,0:T(8,128)(2,1)}, bf16[2,4,384,256]{3,2,1,0:T(8,128)(2,1)S(1)}, u32[]{:S(2)}, u32[]{:S(2)}) collective-permute-start(bf16[2,4,384,256]{3,2,1,0:T(8,128)(2,1)} %get-tuple-element.56), channel_id=1, source_target_pairs={{136,0},{138,2},{140,4},{142,6},{1,9},{3,11},{5,13},{7,15},{152,16... | collective-permute-start | bytes 4718600 | tf_op jit(solution)/shard_map/ppermute | solution.py:53
  140.8 34.1 %collective-permute-start.21 = (bf16[2,4,384,256]{3,2,1,0:T(8,128)(2,1)}, bf16[2,4,384,256]{3,2,1,0:T(8,128)(2,1)S(1)}, u32[]{:S(2)}, u32[]{:S(2)}) collective-permute-start(bf16[2,4,384,256]{3,2,1,0:T(8,128)(2,1)} %get-tuple-element.55), channel_id=1, source_target_pairs={{8,0},{10,2},{12,4},{14,6},{129,9},{131,11},{133,13},{135,15},{24,... | collective-permute-start | bytes 4718600 | tf_op jit(solution)/shard_map/ppermute | solution.py:53
  144.1 19.3 %collective-permute-start.16 = (bf16[4,384,256]{2,1,0:T(8,128)(2,1)S(1)}, bf16[4,384,256]{2,1,0:T(8,128)(2,1)S(1)}, u32[]{:S(2)}, u32[]{:S(2)}) collective-permute-start(bf16[4,384,256]{2,1,0:T(8,128)(2,1)S(1)} %add_convert_fusion.2), channel_id=1, source_target_pairs={{0,6},{1,7},{2,0},{3,1},{4,2},{5,3},{6,4},{7,5},{8,14},{9,15},{10,... | collective-permute-start | bytes 2359304 | tf_op jit(solution)/shard_map/ppermute | solution.py:53
  147.5 19.3 %collective-permute-start.14 = (bf16[4,384,256]{2,1,0:T(8,128)(2,1)S(1)}, bf16[4,384,256]{2,1,0:T(8,128)(2,1)S(1)}, u32[]{:S(2)}, u32[]{:S(2)}) collective-permute-start(bf16[4,384,256]{2,1,0:T(8,128)(2,1)S(1)} %add_convert_fusion.3), channel_id=1, source_target_pairs={{0,2},{1,3},{2,4},{3,5},{4,6},{5,7},{6,0},{7,1},{8,10},{9,11},{10,... | collective-permute-start | bytes 2359304 | tf_op jit(solution)/shard_map/ppermute | solution.py:53
  167.2 16.2 %collective-permute-start.19 = (bf16[2,384,256]{2,1,0:T(8,128)(2,1)S(1)}, bf16[2,384,256]{2,1,0:T(8,128)(2,1)}, u32[]{:S(2)}, u32[]{:S(2)}) collective-permute-start(bf16[2,384,256]{2,1,0:T(8,128)(2,1)S(1)} %get-tuple-element.67), channel_id=1, source_target_pairs={{0,128},{2,130},{4,132},{6,134},{9,137},{11,139},{13,141},{15,143}... | collective-permute-start | bytes 1179656 | tf_op jit(solution)/shard_map/ppermute | solution.py:53
  168.8 14.7 %collective-permute-start.18 = (bf16[2,384,256]{2,1,0:T(8,128)(2,1)S(1)}, bf16[2,384,256]{2,1,0:T(8,128)(2,1)}, u32[]{:S(2)}, u32[]{:S(2)}) collective-permute-start(bf16[2,384,256]{2,1,0:T(8,128)(2,1)S(1)} %get-tuple-element.67), channel_id=1, source_target_pairs={{136,0},{138,2},{140,4},{142,6},{1,9},{3,11},{5,13},{7,15},{152,16... | collective-permute-start | bytes 1179656 | tf_op jit(solution)/shard_map/ppermute | solution.py:53
  180.4 9.4 %collective-permute-start.24 = (bf16[4,384,256]{2,1,0:T(8,128)(2,1)S(1)}, bf16[4,384,256]{2,1,0:T(8,128)(2,1)S(1)}, u32[]{:S(2)}, u32[]{:S(2)}) collective-permute-start(bf16[4,384,256]{2,1,0:T(8,128)(2,1)S(1)} %slice_bitcast_fusion), channel_id=1, source_target_pairs={{0,1},{2,3},{4,5},{6,7},{9,8},{11,10},{13,12},{15,14},{16,17},{18,... | collective-permute-start | bytes 2359304 | tf_op jit(solution)/shard_map/ppermute | solution.py:53
  184.9 11.4 %collective-permute-start.20 = (bf16[384,256]{1,0:T(8,128)(2,1)S(1)}, bf16[384,256]{1,0:T(8,128)(2,1)S(1)}, u32[]{:S(2)}, u32[]{:S(2)}) collective-permute-start(bf16[384,256]{1,0:T(8,128)(2,1)S(1)} %slice_bitcast_fusion.5), channel_id=1, source_target_pairs={{0,1},{2,3},{4,5},{6,7},{9,8},{11,10},{13,12},{15,14},{16,17},{18,... | collective-permute-start | bytes 589832 | tf_op jit(solution)/shard_map/ppermute | solution.py:53
  186.2 10.9 %collective-permute-start.28 = (bf16[1152,256]{1,0:T(8,128)(2,1)S(1)}, bf16[1152,256]{1,0:T(8,128)(2,1)S(1)}, u32[]{:S(2)}, u32[]{:S(2)}) collective-permute-start(bf16[1152,256]{1,0:T(8,128)(2,1)S(1)} %copy-done.12), channel_id=1, source_target_pairs={{8,0},{136,1},{10,2},{138,3},{12,4},{140,5},{14,6},{142,7},{128,8}... | collective-permute-start | bytes 1769480 | tf_op jit(solution)/shard_map/ppermute | solution.py:53
  190.0 10.1 %collective-permute-start.25 = (bf16[384,256]{1,0:T(8,128)(2,1)S(1)}, bf16[384,256]{1,0:T(8,128)(2,1)S(1)}, u32[]{:S(2)}, u32[]{:S(2)}) collective-permute-start(bf16[384,256]{1,0:T(8,128)(2,1)S(1)} %get-tuple-element.63), channel_id=1, source_target_pairs={{0,2},{1,3},{2,4},{3,5},{4,6},{5,7},{6,0},{7,1},{8,10},{9,11},{10,... | collective-permute-start | bytes 589832 | tf_op jit(solution)/shard_map/ppermute | solution.py:53
  191.1 13.0 %collective-permute-start.27 = (bf16[384,256]{1,0:T(8,128)(2,1)S(1)}, bf16[384,256]{1,0:T(8,128)(2,1)S(1)}, u32[]{:S(2)}, u32[]{:S(2)}) collective-permute-start(bf16[384,256]{1,0:T(8,128)(2,1)S(1)} %get-tuple-element.64), channel_id=1, source_target_pairs={{0,4},{1,5},{2,6},{3,7},{4,0},{5,1},{6,2},{7,3},{8,12},{9,13},{10,... | collective-permute-start | bytes 589832 | tf_op jit(solution)/shard_map/ppermute | solution.py:53
  (20 other events, 186.2 us)
Sparse Core Ops, SparseCore 0:
  21.2 62.9 all-gather.2
  119.3 58.3 reduce-scatter.1

commit v3 on v2

--- a/solution.py
+++ b/solution.py
@@ -122,7 +122,7 @@
 
 def projection_kernel(idx, *refs):
     pieces, w = refs[:4], refs[4]
-    far, own, xs, ws, sems = refs[5:]
+    far, own, xs, ws, stage, sems = refs[5:]
     copies = Copies(sems)
     c = idx[I_C]
     features = []
@@ -133,17 +133,20 @@
                 features.append(copies.start(piece.at[pair + slot], xs.at[place, :, block(column(idx, step, slot))]))
         if place == 0:
             weights = [copies.start(w.at[:, pl.ds(256 * p, 256)], ws.at[p]) for p in range(3)]
+    leaving = []
     for place, out in enumerate((far, own)):
         wait(features[8 * place : 8 * place + 8])
         for p in range(3):
             if place == 0:
                 weights[p].wait()
-            out[:, 256 * p : 256 * p + 256] = dot(xs[place], ws[p].reshape(2048, 256))
+            stage[place, :, 256 * p : 256 * p + 256] = dot(xs[place], ws[p].reshape(2048, 256))
+        leaving.append(copies.start(stage.at[place], out))
+    wait(leaving)
 
 
 def projections(idx, x, w):
-    scratch = [pltpu.VMEM((2, 384, 2048), BF), pltpu.VMEM((3, 8, 256, 256), BF)]
-    return call(projection_kernel, [shape(384, 768, dtype=F32)] * 2, scratch, 19, (idx, *x, w), "projections")
+    scratch = [pltpu.VMEM((2, 384, 2048), BF), pltpu.VMEM((3, 8, 256, 256), BF), pltpu.VMEM((2, 384, 768), F32)]
+    return call(projection_kernel, [shape(384, 768, dtype=F32)] * 2, scratch, 21, (idx, *x, w), "projections", ANY)
 
 
 def output_weight_copies(copies, w, dst):
@@ -231,24 +234,27 @@
     return call(weight_grad_kernel, shape(8, 1152, 256), scratch, 26, args, "weight_grads", ANY, (1, 2, 3, 4))
 
 
-def output_kernel(idx, own, other, w, here, up, down, across_up, across_down, hs, os, sems):
+def output_kernel(idx, own, other, w, here, up, down, across_up, across_down, hs, os, stage, sems):
     copies = Copies(sems)
     weights = output_weight_copies(copies, w, os)
     stack_tokens(idx, own, other, hs)
     wait(weights)
-    for step, out in ((0, here), (1, up), (3, down), (2, None)):
+    leaving = []
+    for step, out in ((2, None), (1, up), (3, down), (0, here)):
         for slot in range(4):
-            value = dot(hs[rows_of(token_of(idx, slot))], os[:, block(column(idx, step, slot))]).astype(BF)
-            if out is not None:
-                out[slot] = value
-            else:
-                (across_up, across_down)[slot // 2][slot % 2] = value
+            stage[step, slot] = dot(hs[rows_of(token_of(idx, slot))], os[:, block(column(idx, step, slot))]).astype(BF)
+        if out is None:
+            leaving.append(copies.start(stage.at[step, pl.ds(0, 2)], across_up))
+            leaving.append(copies.start(stage.at[step, pl.ds(2, 2)], across_down))
+        else:
+            leaving.append(copies.start(stage.at[step], out))
+    wait(leaving)
 
 
 def outputs(idx, own, other, w):
     outs = [shape(4, 384, 256)] * 3 + [shape(2, 384, 256)] * 2
-    scratch = [pltpu.VMEM((768, 384), BF), pltpu.VMEM((384, 2048), BF)]
-    return call(output_kernel, outs, scratch, 8, (idx, own, other, w), "outputs", near=(1, 2), traffic=40_000_000)
+    scratch = [pltpu.VMEM((768, 384), BF), pltpu.VMEM((384, 2048), BF), pltpu.VMEM((4, 4, 384, 256), BF)]
+    return call(output_kernel, outs, scratch, 13, (idx, own, other, w), "outputs", ANY, (1, 2), 40_000_000)
 
 
 def input_grad_kernel(idx, own, other, w, first, second, cs, ws, sf, ss, sems):
@@ -262,7 +268,8 @@
             j = column(idx, step, core)
             for pair, (stage, out) in enumerate(((sf, first), (ss, second))):
                 stage[core, step] = dot(cs[rows_of(token_of(idx, 2 * pair))], ws[j], 1, 1).astype(BF)
-                leaving.append(copies.start(stage.at[core, step], out.at[core, step]))
+        for stage, out in ((sf, first), (ss, second)):
+            leaving.append(copies.start(stage.at[:, step], out.at[:, step]))
     wait(leaving)
 
 

time: 212 us -> 212 us (level)
  no operation moved by 1% of the time
where the time goes in v3:
time: 212 us
  waiting for transfers between devices  79 us (37%)
  starting transfers between devices  60.8 us (29%)
  Pallas kernels  43.2 us (20%)
  between operations  14.4 us (7%)
  local copies, waits for them, and re-layouts  7.73 us (4%)
  other arithmetic  6.67 us (3%)
    ppermute x29, waiting for transfers between devices, move(): return lax.ppermute(value, AXES, pairs)  71.2 us
    ppermute x29, starting transfers between devices, move(): return lax.ppermute(value, AXES, pairs)  60.7 us
    pallas_call x5, Pallas kernels, call(): pl.pallas_call(kernel, out_shape=outs, in_specs=[SMEM] + [VMEM if i in ne...  35.7 us
    all_gather x1, waiting for transfers between devices, per_device(): w = lax.all_gather(shard, 'dp', axis_index_groups=Z_GROUPS)  7.76 us
    convert_element_type x6, other arithmetic, add(): return functools.reduce(jnp.add, [t.astype(F32) for t in terms]).astype(BF)  4.77 us
  transfers between devices with their start and end apart: 31, of which 15 were waited for; matrix products, arithmetic and copies ran while one was open for 5% of the time, Pallas kernels for 13%

profile of v3, /device:TPU:1, one launch (start us, length us, event | category | flops | bytes accessed | tf_op | source)
XLA Modules:
  0.0 211.7 jit_solution(16840497207223463255)
XLA Ops:
  9.2 3.9 %collective-permute-start = (bf16[1152,256]{1,0:T(8,128)(2,1)}, bf16[1152,256]{1,0:T(8,128)(2,1)S(1)}, u32[]{:S(2)}, u32[]{:S(2)}) collective-permute-start(bf16[1152,256]{1,0:T(8,128)(2,1)} %pack.1), channel_id=1, source_target_pairs={{0,8},{1,136},{2,10},{3,138},{4,12},{5,140},{6,14},{7,142},{8,128}... | collective-permute-start | bytes 1769480 | tf_op jit(solution)/shard_map/ppermute | solution.py:53
  16.6 3.6 %collective-permute-done = bf16[1152,256]{1,0:T(8,128)(2,1)S(1)} collective-permute-done((bf16[1152,256]{1,0:T(8,128)(2,1)}, bf16[1152,256]{1,0:T(8,128)(2,1)S(1)}, u32[]{:S(2)}, u32[]{:S(2)}) %collective-permute-start) | collective-permute-done | bytes 589856 | tf_op jit(solution)/shard_map/ppermute | solution.py:53
  24.4 2.8 %constant_dynamic-slice_fusion = bf16[384,2048]{1,0:T(8,128)(2,1)} fusion(bf16[384,4096]{1,0:T(8,128)(2,1)} %local.3, s32[]{:T(128)S(6)} %select_n.70), kind=kLoop, calls=%fused_computation.22 | loop fusion | bytes 3145732 | tf_op jit(solution)/shard_map/dynamic_slice | solution.py:329
  27.3 3.6 %collective-permute-done.2 = bf16[2,384,256]{2,1,0:T(8,128)(2,1)S(1)} collective-permute-done((bf16[2,384,256]{2,1,0:T(8,128)(2,1)S(1)}, bf16[2,384,256]{2,1,0:T(8,128)(2,1)S(1)}, u32[]{:S(2)}, u32[]{:S(2)}) %collective-permute-start.2) | collective-permute-done | bytes 393248 | tf_op jit(solution)/shard_map/ppermute | solution.py:53
  31.7 6.8 %collective-permute-start.9 = (bf16[384,2048]{1,0:T(8,128)(2,1)}, bf16[384,2048]{1,0:T(8,128)(2,1)}, u32[]{:S(2)}, u32[]{:S(2)}) collective-permute-start(bf16[384,2048]{1,0:T(8,128)(2,1)} %constant_dynamic-slice_fusion), channel_id=1, source_target_pairs={{0,136},{1,137},{2,138},{3,139},{4,140},{5,141},{6,142},{7,143},{8... | collective-permute-start | bytes 4718600 | tf_op jit(solution)/shard_map/ppermute | solution.py:53
  38.5 2.9 %collective-permute-start.7 = (bf16[4,384,256]{2,1,0:T(8,128)(2,1)S(1)}, bf16[4,384,256]{2,1,0:T(8,128)(2,1)S(1)}, u32[]{:S(2)}, u32[]{:S(2)}) collective-permute-start(bf16[4,384,256]{2,1,0:T(8,128)(2,1)S(1)} %pad_maximum_fusion.refs_0_), channel_id=1, source_target_pairs={{0,4},{1,5},{2,6},{3,7},{4,0},{5,1},{6,2},{7,3},{8,12},{9,13},{10,... | collective-permute-start | bytes 2359304 | tf_op jit(solution)/shard_map/ppermute | solution.py:53
  43.5 12.3 %collective-permute-done.7.refs_3_ = bf16[4,384,256]{2,1,0:T(8,128)(2,1)S(1)} collective-permute-done((bf16[4,384,256]{2,1,0:T(8,128)(2,1)S(1)}, bf16[4,384,256]{2,1,0:T(8,128)(2,1)S(1)}, u32[]{:S(2)}, u32[]{:S(2)}) %collective-permute-start.7) | collective-permute-done | bytes 786464 | tf_op jit(solution)/shard_map/ppermute | solution.py:53
  55.9 19.8 %collective-permute-done.6.refs_2_ = bf16[4,384,256]{2,1,0:T(8,128)(2,1)S(1)} collective-permute-done((bf16[4,384,256]{2,1,0:T(8,128)(2,1)S(1)}, bf16[4,384,256]{2,1,0:T(8,128)(2,1)S(1)}, u32[]{:S(2)}, u32[]{:S(2)}) %collective-permute-start.6) | collective-permute-done | bytes 786464 | tf_op jit(solution)/shard_map/ppermute | solution.py:53
  76.4 7.8 %all-gather.3.cloned.1.call-done = bf16[9216,256]{1,0:T(8,128)(2,1)} async-done(((bf16[1152,256]{1,0:T(8,128)(2,1)}), bf16[9216,256]{1,0:T(8,128)(2,1)}) %all-gather.3.cloned.1.call-update) | async-done | bytes 4718608 | tf_op jit(solution)/shard_map/all_gather | solution.py:327
  84.2 8.4 %projections.1 = (f32[384,768]{1,0:T(8,128)}, f32[384,768]{1,0:T(8,128)}) custom-call(s32[6]{0:T(128)} %stack.36.idx, bf16[4,384,256]{2,1,0:T(8,128)(2,1)} %copy-done, bf16[4,384,256]{2,1,0:T(8,128)(2,1)} %copy-done.3, bf16[4,384,256]{2,1,0:T(8,128)(2,1)} %copy-done.2, bf16[4,384,256]{2,1,0:T(8,128)(2,1)} %copy-done.1, bf16[8,1152,256]{2,1,0:T(8,128)(2,1)} %bitcast.31), custom_call_target="tpu_custom_call" | custom-call | flops 1000 | bytes 1000 | tf_op jit(solution)/shard_map/projections/pallas_call | solution.py:95
  93.4 5.7 %hidden_cots.1 = (f32[384,384]{1,0:T(8,128)}, f32[384,384]{1,0:T(8,128)}) custom-call(s32[6]{0:T(128)} %stack.36.idx, bf16[384,4096]{1,0:T(8,128)(2,1)} %local.3, bf16[384,2048]{1,0:T(8,128)(2,1)} %collective-permute-done.9.remote, bf16[8,1152,256]{2,1,0:T(8,128)(2,1)} %bitcast.32), custom_call_target="tpu_custom_call" | custom-call | flops 1000 | bytes 1000 | tf_op jit(solution)/shard_map/hidden_cots/pallas_call | solution.py:95
  102.2 3.3 %activation.1 = (bf16[384,384]{1,0:T(8,128)(2,1)}, bf16[384,768]{1,0:T(8,128)(2,1)}) custom-call(f32[384,768]{1,0:T(8,128)} %get-tuple-element.39.own, f32[384,768]{1,0:T(8,128)} %collective-permute-done.8.far, f32[384,384]{1,0:T(8,128)} %get-tuple-element.42.hc_own, f32[384,384]{1,0:T(8,128)} %copy-done.9), custom_call_target="tpu_custom_call" | custom-call | flops 1000 | bytes 1000 | tf_op jit(solution)/shard_map/activation/pallas_call | solution.py:191
  109.7 9.4 %weight_grads.1 = bf16[8,1152,256]{2,1,0:T(8,128)(2,1)} custom-call(s32[6]{0:T(128)} %stack.36.idx, bf16[384,384]{1,0:T(8,128)(2,1)} %get-tuple-element.44.hidden.own, bf16[384,384]{1,0:T(8,128)(2,1)} %copy-done.6, bf16[384,768]{1,0:T(8,128)(2,1)} %get-tuple-element.45.cots.own, bf16[384,768]{1,0:T(8,128)(2,1)} %copy-done.4, bf16[384,4096]{1,0:T(8,128)(2,1)} %local.3, ...), custom_call_target="tpu_custom_call" | custom-call | flops 1000 | bytes 1000 | tf_op jit(solution)/shard_map/weight_grads/pallas_call | solution.py:95
  119.2 6.8 %input_grads.1 = (bf16[2,4,384,256]{3,2,1,0:T(8,128)(2,1)}, bf16[2,4,384,256]{3,2,1,0:T(8,128)(2,1)}) custom-call(s32[6]{0:T(128)} %stack.36.idx, bf16[384,768]{1,0:T(8,128)(2,1)} %get-tuple-element.45.cots.own, bf16[384,768]{1,0:T(8,128)(2,1)} %copy-done.4, bf16[8,1152,256]{2,1,0:T(8,128)(2,1)} %bitcast.33), custom_call_target="tpu_custom_call" | custom-call | flops 1000 | bytes 1000 | tf_op jit(solution)/shard_map/input_grads/pallas_call | solution.py:95
  126.1 5.4 %outputs.1 = (bf16[4,384,256]{2,1,0:T(8,128)(2,1)}, bf16[4,384,256]{2,1,0:T(8,128)(2,1)}, bf16[4,384,256]{2,1,0:T(8,128)(2,1)}, bf16[2,384,256]{2,1,0:T(8,128)(2,1)}, bf16[2,384,256]{2,1,0:T(8,128)(2,1)}) custom-call(s32[6]{0:T(128)} %stack.36.idx, bf16[384,384]{1,0:T(8,128)(2,1)} %get-tuple-element.44.hidden.own, bf16[384,384]{1,0:T(8,128)(2,1)} %copy-done.6, ...), custom_call_target="tpu_custom_call" | custom-call | flops 1000 | bytes 40000000 | tf_op jit(solution)/shard_map/outputs/pallas_call | solution.py:95
  134.7 6.1 %collective-permute-start.22 = (bf16[2,4,384,256]{3,2,1,0:T(8,128)(2,1)}, bf16[2,4,384,256]{3,2,1,0:T(8,128)(2,1)S(1)}, u32[]{:S(2)}, u32[]{:S(2)}) collective-permute-start(bf16[2,4,384,256]{3,2,1,0:T(8,128)(2,1)} %get-tuple-element.56), channel_id=1, source_target_pairs={{136,0},{138,2},{140,4},{142,6},{1,9},{3,11},{5,13},{7,15},{152,16... | collective-permute-start | bytes 4718600 | tf_op jit(solution)/shard_map/ppermute | solution.py:53
  144.1 3.4 %collective-permute-start.16 = (bf16[4,384,256]{2,1,0:T(8,128)(2,1)S(1)}, bf16[4,384,256]{2,1,0:T(8,128)(2,1)S(1)}, u32[]{:S(2)}, u32[]{:S(2)}) collective-permute-start(bf16[4,384,256]{2,1,0:T(8,128)(2,1)S(1)} %add_convert_fusion.2), channel_id=1, source_target_pairs={{0,6},{1,7},{2,0},{3,1},{4,2},{5,3},{6,4},{7,5},{8,14},{9,15},{10,... | collective-permute-start | bytes 2359304 | tf_op jit(solution)/shard_map/ppermute | solution.py:53
  147.7 15.8 %collective-permute-done.16 = bf16[4,384,256]{2,1,0:T(8,128)(2,1)S(1)} collective-permute-done((bf16[4,384,256]{2,1,0:T(8,128)(2,1)S(1)}, bf16[4,384,256]{2,1,0:T(8,128)(2,1)S(1)}, u32[]{:S(2)}, u32[]{:S(2)}) %collective-permute-start.16) | collective-permute-done | bytes 786464 | tf_op jit(solution)/shard_map/ppermute | solution.py:53
  163.5 3.4 %collective-permute-done.14 = bf16[4,384,256]{2,1,0:T(8,128)(2,1)S(1)} collective-permute-done((bf16[4,384,256]{2,1,0:T(8,128)(2,1)S(1)}, bf16[4,384,256]{2,1,0:T(8,128)(2,1)S(1)}, u32[]{:S(2)}, u32[]{:S(2)}) %collective-permute-start.14) | collective-permute-done | bytes 786464 | tf_op jit(solution)/shard_map/ppermute | solution.py:53
  168.8 6.2 %collective-permute-start.18 = (bf16[2,384,256]{2,1,0:T(8,128)(2,1)S(1)}, bf16[2,384,256]{2,1,0:T(8,128)(2,1)}, u32[]{:S(2)}, u32[]{:S(2)}) collective-permute-start(bf16[2,384,256]{2,1,0:T(8,128)(2,1)S(1)} %get-tuple-element.67), channel_id=1, source_target_pairs={{136,0},{138,2},{140,4},{142,6},{1,9},{3,11},{5,13},{7,15},{152,16... | collective-permute-start | bytes 1179656 | tf_op jit(solution)/shard_map/ppermute | solution.py:53
  175.0 4.6 %collective-permute-start.17 = (bf16[2,384,256]{2,1,0:T(8,128)(2,1)S(1)}, bf16[2,384,256]{2,1,0:T(8,128)(2,1)}, u32[]{:S(2)}, u32[]{:S(2)}) collective-permute-start(bf16[2,384,256]{2,1,0:T(8,128)(2,1)S(1)} %get-tuple-element.66), channel_id=1, source_target_pairs={{8,0},{10,2},{12,4},{14,6},{129,9},{131,11},{133,13},{135,15},{24,... | collective-permute-start | bytes 1179656 | tf_op jit(solution)/shard_map/ppermute | solution.py:53
  186.3 3.7 %collective-permute-start.28 = (bf16[1152,256]{1,0:T(8,128)(2,1)S(1)}, bf16[1152,256]{1,0:T(8,128)(2,1)S(1)}, u32[]{:S(2)}, u32[]{:S(2)}) collective-permute-start(bf16[1152,256]{1,0:T(8,128)(2,1)S(1)} %copy-done.12), channel_id=1, source_target_pairs={{8,0},{136,1},{10,2},{138,3},{12,4},{140,5},{14,6},{142,7},{128,8}... | collective-permute-start | bytes 1769480 | tf_op jit(solution)/shard_map/ppermute | solution.py:53
  191.1 4.8 %collective-permute-start.27 = (bf16[384,256]{1,0:T(8,128)(2,1)S(1)}, bf16[384,256]{1,0:T(8,128)(2,1)S(1)}, u32[]{:S(2)}, u32[]{:S(2)}) collective-permute-start(bf16[384,256]{1,0:T(8,128)(2,1)S(1)} %get-tuple-element.64), channel_id=1, source_target_pairs={{0,4},{1,5},{2,6},{3,7},{4,0},{5,1},{6,2},{7,3},{8,12},{9,13},{10,... | collective-permute-start | bytes 589832 | tf_op jit(solution)/shard_map/ppermute | solution.py:53
  200.2 3.9 %collective-permute-done.27 = bf16[384,256]{1,0:T(8,128)(2,1)S(1)} collective-permute-done((bf16[384,256]{1,0:T(8,128)(2,1)S(1)}, bf16[384,256]{1,0:T(8,128)(2,1)S(1)}, u32[]{:S(2)}, u32[]{:S(2)}) %collective-permute-start.27) | collective-permute-done | bytes 196640 | tf_op jit(solution)/shard_map/ppermute | solution.py:53
  (92 shorter events, 43.1 us)
Async XLA Ops:
  7.2 77.0 %all-gather.3.cloned.1.call-start = ((), (), s32[]{:S(2)}) async-start(), calls=%async_computation.2 | async-start | bytes 5308416 | tf_op jit(solution)/shard_map/all_gather | solution.py:327
  9.2 11.0 %collective-permute-start = (bf16[1152,256]{1,0:T(8,128)(2,1)}, bf16[1152,256]{1,0:T(8,128)(2,1)S(1)}, u32[]{:S(2)}, u32[]{:S(2)}) collective-permute-start(bf16[1152,256]{1,0:T(8,128)(2,1)} %pack.1), channel_id=1, source_target_pairs={{0,8},{1,136},{2,10},{3,138},{4,12},{5,140},{6,14},{7,142},{8,128}... | collective-permute-start | bytes 1769480 | tf_op jit(solution)/shard_map/ppermute | solution.py:53
  21.1 159.4 %reduce-scatter.2.cloned.1.call-start = ((), (), s32[]{:S(2)}) async-start(), calls=%async_computation.1 | async-start | bytes 5308416 | tf_op jit(solution)/shard_map/reduce_scatter | solution.py:346
  21.1 9.7 %collective-permute-start.2 = (bf16[2,384,256]{2,1,0:T(8,128)(2,1)S(1)}, bf16[2,384,256]{2,1,0:T(8,128)(2,1)S(1)}, u32[]{:S(2)}, u32[]{:S(2)}) collective-permute-start(bf16[2,384,256]{2,1,0:T(8,128)(2,1)S(1)} %pad_maximum_fusion.1), channel_id=1, source_target_pairs={{0,8},{2,10},{4,12},{6,14},{9,129},{11,131},{13,133},{15,135},{16,... | collective-permute-start | bytes 1179656 | tf_op jit(solution)/shard_map/ppermute | solution.py:53
  22.4 9.1 %collective-permute-start.4 = (bf16[2,384,256]{2,1,0:T(8,128)(2,1)S(1)}, bf16[2,384,256]{2,1,0:T(8,128)(2,1)S(1)}, u32[]{:S(2)}, u32[]{:S(2)}) collective-permute-start(bf16[2,384,256]{2,1,0:T(8,128)(2,1)S(1)} %pad_maximum_fusion.1), channel_id=1, source_target_pairs={{0,136},{2,138},{4,140},{6,142},{9,1},{11,3},{13,5},{15,7},{16,152... | collective-permute-start | bytes 1179656 | tf_op jit(solution)/shard_map/ppermute | solution.py:53
  31.7 61.6 %collective-permute-start.9 = (bf16[384,2048]{1,0:T(8,128)(2,1)}, bf16[384,2048]{1,0:T(8,128)(2,1)}, u32[]{:S(2)}, u32[]{:S(2)}) collective-permute-start(bf16[384,2048]{1,0:T(8,128)(2,1)} %constant_dynamic-slice_fusion), channel_id=1, source_target_pairs={{0,136},{1,137},{2,138},{3,139},{4,140},{5,141},{6,142},{7,143},{8... | collective-permute-start | bytes 4718600 | tf_op jit(solution)/shard_map/ppermute | solution.py:53
  38.5 17.3 %collective-permute-start.7 = (bf16[4,384,256]{2,1,0:T(8,128)(2,1)S(1)}, bf16[4,384,256]{2,1,0:T(8,128)(2,1)S(1)}, u32[]{:S(2)}, u32[]{:S(2)}) collective-permute-start(bf16[4,384,256]{2,1,0:T(8,128)(2,1)S(1)} %pad_maximum_fusion.refs_0_), channel_id=1, source_target_pairs={{0,4},{1,5},{2,6},{3,7},{4,0},{5,1},{6,2},{7,3},{8,12},{9,13},{10,... | collective-permute-start | bytes 2359304 | tf_op jit(solution)/shard_map/ppermute | solution.py:53
  41.4 34.2 %collective-permute-start.6 = (bf16[4,384,256]{2,1,0:T(8,128)(2,1)S(1)}, bf16[4,384,256]{2,1,0:T(8,128)(2,1)S(1)}, u32[]{:S(2)}, u32[]{:S(2)}) collective-permute-start(bf16[4,384,256]{2,1,0:T(8,128)(2,1)S(1)} %pad_maximum_fusion.refs_0_), channel_id=1, source_target_pairs={{0,6},{1,7},{2,0},{3,1},{4,2},{5,3},{6,4},{7,5},{8,14},{9,15},{10,... | collective-permute-start | bytes 2359304 | tf_op jit(solution)/shard_map/ppermute | solution.py:53
  42.2 34.2 %collective-permute-start.5 = (bf16[4,384,256]{2,1,0:T(8,128)(2,1)S(1)}, bf16[4,384,256]{2,1,0:T(8,128)(2,1)S(1)}, u32[]{:S(2)}, u32[]{:S(2)}) collective-permute-start(bf16[4,384,256]{2,1,0:T(8,128)(2,1)S(1)} %pad_maximum_fusion.refs_0_), channel_id=1, source_target_pairs={{0,2},{1,3},{2,4},{3,5},{4,6},{5,7},{6,0},{7,1},{8,10},{9,11},{10,... | collective-permute-start | bytes 2359304 | tf_op jit(solution)/shard_map/ppermute | solution.py:53
  92.6 8.7 %collective-permute-start.8 = (f32[384,768]{1,0:T(8,128)}, f32[384,768]{1,0:T(8,128)}, u32[]{:S(2)}, u32[]{:S(2)}) collective-permute-start(f32[384,768]{1,0:T(8,128)} %get-tuple-element.40), channel_id=1, source_target_pairs={{0,1},{1,0},{2,3},{3,2},{4,5},{5,4},{6,7},{7,6},{8,9},{9,8},{10,11... | collective-permute-start | bytes 3538952 | tf_op jit(solution)/shard_map/ppermute | solution.py:53
  131.4 11.3 %collective-permute-start.15 = (bf16[2,384,256]{2,1,0:T(8,128)(2,1)}, bf16[2,384,256]{2,1,0:T(8,128)(2,1)S(1)}, u32[]{:S(2)}, u32[]{:S(2)}) collective-permute-start(bf16[2,384,256]{2,1,0:T(8,128)(2,1)} %get-tuple-element.54), channel_id=1, source_target_pairs={{0,6},{1,7},{2,0},{3,1},{4,2},{5,3},{6,4},{7,5},{8,14},{9,15},{10,... | collective-permute-start | bytes 1179656 | tf_op jit(solution)/shard_map/ppermute | solution.py:53
  134.0 13.5 %collective-permute-start.13 = (bf16[2,384,256]{2,1,0:T(8,128)(2,1)}, bf16[2,384,256]{2,1,0:T(8,128)(2,1)S(1)}, u32[]{:S(2)}, u32[]{:S(2)}) collective-permute-start(bf16[2,384,256]{2,1,0:T(8,128)(2,1)} %get-tuple-element.52), channel_id=1, source_target_pairs={{0,2},{1,3},{2,4},{3,5},{4,6},{5,7},{6,0},{7,1},{8,10},{9,11},{10,... | collective-permute-start | bytes 1179656 | tf_op jit(solution)/shard_map/ppermute | solution.py:53
  134.0 45.6 %collective-permute-start.23 = (bf16[2,4,384,256]{3,2,1,0:T(8,128)(2,1)}, bf16[2,4,384,256]{3,2,1,0:T(8,128)(2,1)S(1)}, u32[]{:S(2)}, u32[]{:S(2)}) collective-permute-start(bf16[2,4,384,256]{3,2,1,0:T(8,128)(2,1)} %get-tuple-element.56), channel_id=1, source_target_pairs={{0,128},{2,130},{4,132},{6,134},{9,137},{11,139},{13,141},{15,143}... | collective-permute-start | bytes 4718600 | tf_op jit(solution)/shard_map/ppermute | solution.py:53
  134.7 44.8 %collective-permute-start.22 = (bf16[2,4,384,256]{3,2,1,0:T(8,128)(2,1)}, bf16[2,4,384,256]{3,2,1,0:T(8,128)(2,1)S(1)}, u32[]{:S(2)}, u32[]{:S(2)}) collective-permute-start(bf16[2,4,384,256]{3,2,1,0:T(8,128)(2,1)} %get-tuple-element.56), channel_id=1, source_target_pairs={{136,0},{138,2},{140,4},{142,6},{1,9},{3,11},{5,13},{7,15},{152,16... | collective-permute-start | bytes 4718600 | tf_op jit(solution)/shard_map/ppermute | solution.py:53
  140.9 34.1 %collective-permute-start.21 = (bf16[2,4,384,256]{3,2,1,0:T(8,128)(2,1)}, bf16[2,4,384,256]{3,2,1,0:T(8,128)(2,1)S(1)}, u32[]{:S(2)}, u32[]{:S(2)}) collective-permute-start(bf16[2,4,384,256]{3,2,1,0:T(8,128)(2,1)} %get-tuple-element.55), channel_id=1, source_target_pairs={{8,0},{10,2},{12,4},{14,6},{129,9},{131,11},{133,13},{135,15},{24,... | collective-permute-start | bytes 4718600 | tf_op jit(solution)/shard_map/ppermute | solution.py:53
  144.1 19.4 %collective-permute-start.16 = (bf16[4,384,256]{2,1,0:T(8,128)(2,1)S(1)}, bf16[4,384,256]{2,1,0:T(8,128)(2,1)S(1)}, u32[]{:S(2)}, u32[]{:S(2)}) collective-permute-start(bf16[4,384,256]{2,1,0:T(8,128)(2,1)S(1)} %add_convert_fusion.2), channel_id=1, source_target_pairs={{0,6},{1,7},{2,0},{3,1},{4,2},{5,3},{6,4},{7,5},{8,14},{9,15},{10,... | collective-permute-start | bytes 2359304 | tf_op jit(solution)/shard_map/ppermute | solution.py:53
  147.6 19.3 %collective-permute-start.14 = (bf16[4,384,256]{2,1,0:T(8,128)(2,1)S(1)}, bf16[4,384,256]{2,1,0:T(8,128)(2,1)S(1)}, u32[]{:S(2)}, u32[]{:S(2)}) collective-permute-start(bf16[4,384,256]{2,1,0:T(8,128)(2,1)S(1)} %add_convert_fusion.3), channel_id=1, source_target_pairs={{0,2},{1,3},{2,4},{3,5},{4,6},{5,7},{6,0},{7,1},{8,10},{9,11},{10,... | collective-permute-start | bytes 2359304 | tf_op jit(solution)/shard_map/ppermute | solution.py:53
  167.3 16.2 %collective-permute-start.19 = (bf16[2,384,256]{2,1,0:T(8,128)(2,1)S(1)}, bf16[2,384,256]{2,1,0:T(8,128)(2,1)}, u32[]{:S(2)}, u32[]{:S(2)}) collective-permute-start(bf16[2,384,256]{2,1,0:T(8,128)(2,1)S(1)} %get-tuple-element.67), channel_id=1, source_target_pairs={{0,128},{2,130},{4,132},{6,134},{9,137},{11,139},{13,141},{15,143}... | collective-permute-start | bytes 1179656 | tf_op jit(solution)/shard_map/ppermute | solution.py:53
  168.8 14.7 %collective-permute-start.18 = (bf16[2,384,256]{2,1,0:T(8,128)(2,1)S(1)}, bf16[2,384,256]{2,1,0:T(8,128)(2,1)}, u32[]{:S(2)}, u32[]{:S(2)}) collective-permute-start(bf16[2,384,256]{2,1,0:T(8,128)(2,1)S(1)} %get-tuple-element.67), channel_id=1, source_target_pairs={{136,0},{138,2},{140,4},{142,6},{1,9},{3,11},{5,13},{7,15},{152,16... | collective-permute-start | bytes 1179656 | tf_op jit(solution)/shard_map/ppermute | solution.py:53
  180.5 9.4 %collective-permute-start.24 = (bf16[4,384,256]{2,1,0:T(8,128)(2,1)S(1)}, bf16[4,384,256]{2,1,0:T(8,128)(2,1)S(1)}, u32[]{:S(2)}, u32[]{:S(2)}) collective-permute-start(bf16[4,384,256]{2,1,0:T(8,128)(2,1)S(1)} %slice_bitcast_fusion), channel_id=1, source_target_pairs={{0,1},{2,3},{4,5},{6,7},{9,8},{11,10},{13,12},{15,14},{16,17},{18,... | collective-permute-start | bytes 2359304 | tf_op jit(solution)/shard_map/ppermute | solution.py:53
  185.0 11.4 %collective-permute-start.20 = (bf16[384,256]{1,0:T(8,128)(2,1)S(1)}, bf16[384,256]{1,0:T(8,128)(2,1)S(1)}, u32[]{:S(2)}, u32[]{:S(2)}) collective-permute-start(bf16[384,256]{1,0:T(8,128)(2,1)S(1)} %slice_bitcast_fusion.5), channel_id=1, source_target_pairs={{0,1},{2,3},{4,5},{6,7},{9,8},{11,10},{13,12},{15,14},{16,17},{18,... | collective-permute-start | bytes 589832 | tf_op jit(solution)/shard_map/ppermute | solution.py:53
  186.3 10.9 %collective-permute-start.28 = (bf16[1152,256]{1,0:T(8,128)(2,1)S(1)}, bf16[1152,256]{1,0:T(8,128)(2,1)S(1)}, u32[]{:S(2)}, u32[]{:S(2)}) collective-permute-start(bf16[1152,256]{1,0:T(8,128)(2,1)S(1)} %copy-done.12), channel_id=1, source_target_pairs={{8,0},{136,1},{10,2},{138,3},{12,4},{140,5},{14,6},{142,7},{128,8}... | collective-permute-start | bytes 1769480 | tf_op jit(solution)/shard_map/ppermute | solution.py:53
  190.1 10.1 %collective-permute-start.25 = (bf16[384,256]{1,0:T(8,128)(2,1)S(1)}, bf16[384,256]{1,0:T(8,128)(2,1)S(1)}, u32[]{:S(2)}, u32[]{:S(2)}) collective-permute-start(bf16[384,256]{1,0:T(8,128)(2,1)S(1)} %get-tuple-element.63), channel_id=1, source_target_pairs={{0,2},{1,3},{2,4},{3,5},{4,6},{5,7},{6,0},{7,1},{8,10},{9,11},{10,... | collective-permute-start | bytes 589832 | tf_op jit(solution)/shard_map/ppermute | solution.py:53
  191.1 13.0 %collective-permute-start.27 = (bf16[384,256]{1,0:T(8,128)(2,1)S(1)}, bf16[384,256]{1,0:T(8,128)(2,1)S(1)}, u32[]{:S(2)}, u32[]{:S(2)}) collective-permute-start(bf16[384,256]{1,0:T(8,128)(2,1)S(1)} %get-tuple-element.64), channel_id=1, source_target_pairs={{0,4},{1,5},{2,6},{3,7},{4,0},{5,1},{6,2},{7,3},{8,12},{9,13},{10,... | collective-permute-start | bytes 589832 | tf_op jit(solution)/shard_map/ppermute | solution.py:53
  (20 other events, 186.3 us)
Sparse Core Ops, SparseCore 0:
  21.2 62.9 all-gather.2
  119.3 58.3 reduce-scatter.1
